TPU v7x, 32 devices: a whole 2x2x4 slice. The times are simulated.
32 devices in a mesh: seq: 8 (over y, x, core), mp: 4 (over z).
Axes of the slice: x: 2, y: 2, z: 4, core: 2. Of those that a mesh axis runs over, the one named last changes fastest.
Arguments:
- tokens: bfloat16 [2, 2048, 2048], P(None, ('seq', 'mp')), may hold values from -6 to 6
- lengths: int32 [2], replicated, may hold values from 512 to 2048, as said below
- mixer_gain: float32 [2048], replicated, may hold values from 0.5 to 1.5
- query_weight: bfloat16 [2048, 2048], P('seq', 'mp'), may hold values from -0.125 to 0.125
- key_weight: bfloat16 [2048, 2048], P('seq', 'mp'), may hold values from -0.125 to 0.125
- value_weight: bfloat16 [2048, 2048], P('seq', 'mp'), may hold values from -0.125 to 0.125
- beta_weight: bfloat16 [2048, 16], P('seq', 'mp'), may hold values from -0.125 to 0.125
- beta_bias: float32 [16], replicated, may hold values from -4.5 to -1.5
- conv_weight: float32 [3, 4, 2048], replicated, may hold values from -0.6 to 0.6
- head_gain: float32 [128], replicated, may hold values from 0.5 to 1.5
- out_weight: bfloat16 [2048, 2048], P('mp', 'seq'), may hold values from -0.125 to 0.125
- feed_gain: float32 [2048], replicated, may hold values from 0.5 to 1.5
- gate_weight: bfloat16 [2048, 5632], P('seq', 'mp'), may hold values from -0.125 to 0.125
- up_weight: bfloat16 [2048, 5632], P('seq', 'mp'), may hold values from -0.125 to 0.125
- down_weight: bfloat16 [5632, 2048], P('mp', 'seq'), may hold values from -0.078125 to 0.078125
- cotangent: bfloat16 [2, 2048, 2048], P(None, ('seq', 'mp')), may hold values from -6 to 6
Outputs:
- block_output: float32 [2, 2048, 2048], P(None, ('seq', 'mp'))
- grad_tokens: float32 [2, 2048, 2048], P(None, ('seq', 'mp'))
- grad_mixer_gain: float32 [2048], replicated
- grad_query_weight: float32 [2048, 2048], P('seq', 'mp')
- grad_key_weight: float32 [2048, 2048], P('seq', 'mp')
- grad_value_weight: float32 [2048, 2048], P('seq', 'mp')
- grad_beta_weight: float32 [2048, 16], P('seq', 'mp')
- grad_beta_bias: float32 [16], replicated
- grad_conv_weight: float32 [3, 4, 2048], replicated
- grad_head_gain: float32 [128], replicated
- grad_out_weight: float32 [2048, 2048], P('mp', 'seq')
- grad_feed_gain: float32 [2048], replicated
- grad_gate_weight: float32 [2048, 5632], P('seq', 'mp')
- grad_up_weight: float32 [2048, 5632], P('seq', 'mp')
- grad_down_weight: float32 [5632, 2048], P('mp', 'seq')
- state_norm: float32 [], replicated
Inputs may be any that keep to these rules, and one draw needn't show every extreme that they name: `lengths`: each length is at least 512; one sequence, drawn from the seed, has exactly 2048 valid positions.
All inputs are finite; a program needn't handle non-finite values.
Results may differ from a plain program's by a relative error of at most 0.0099.
Values may be sent and summed in bfloat16 or wider, within the bound.
A program may use at most 320 MiB of HBM per device.

v0:
```python
import jax
import jax.numpy as jnp
from jax import lax
from jax.sharding import PartitionSpec as P

HEADS = 16
HEAD_DIM = 128
BLOCK = 64
NSEQ = 2


EPSILON = 1e-05
HIGHEST = lax.Precision.HIGHEST


def passed_along(block, axis, distance):
    devices = range(lax.axis_size(axis))
    route = [(i - distance, i) for i in devices if i - distance in devices]
    return lax.ppermute(block, axis, route)


def entering_2(x, axis, combine, identity, reverse):
    devices, mine = (lax.axis_size(axis), lax.axis_index(axis))
    everything = jax.tree.map(lambda part: lax.all_gather(part, axis), x)
    start = jax.tree.map(
        lambda part, zero: jnp.broadcast_to(jnp.asarray(zero, part.dtype), part.shape), x, identity
    )

    def lap(k, before):
        at = devices - 1 - k if reverse else k
        reached = at > mine if reverse else at < mine
        new = combine(before, jax.tree.map(lambda part: part[at], everything))
        return jax.tree.map(lambda a, b: jnp.where(reached, a, b), new, before)

    return lax.fori_loop(0, devices, lap, start)


def matmul_high(left, right):
    return jnp.matmul(left, right, precision=HIGHEST)


def row_scale(values):
    return lax.rsqrt(jnp.mean(values * values, -1, keepdims=True) + EPSILON)


def norm_backward(grad_normed, unit_rows, scale):
    return scale * (grad_normed - unit_rows * jnp.mean(grad_normed * unit_rows, -1, keepdims=True))


def block_terms(keys, values, betas):
    size = keys.shape[-2]
    identity_mat = jnp.eye(size, dtype=jnp.float32)
    gram = jnp.einsum("...id,...jd->...ij", keys, keys, precision=HIGHEST)
    lower = jnp.tril(gram * betas[..., :, None], -1)
    inverse = identity_mat - lower
    power = lower
    covered = 2
    while covered < size:
        power = matmul_high(power, power)
        inverse = matmul_high(inverse, identity_mat + power)
        covered = covered * 2
    return (
        matmul_high(inverse, keys * betas[..., None]),
        matmul_high(inverse, values * betas[..., None]),
    )


def apply_terms(carried, queries, keys, weighted_keys, weighted_values):
    fresh = weighted_values - matmul_high(weighted_keys, carried)
    scores = jnp.tril(jnp.einsum("...id,...jd->...ij", queries, keys, precision=HIGHEST))
    output = matmul_high(queries, carried) + matmul_high(scores, fresh)
    carried = carried + matmul_high(jnp.swapaxes(keys, -1, -2), fresh)
    return (output, carried)


def block_advance(carried, queries, keys, values, betas):
    weighted_keys, weighted_values = block_terms(keys, values, betas)
    return apply_terms(carried, queries, keys, weighted_keys, weighted_values)


def prepare(extended, conv_local, logits, bias_local, live_mask):
    taps = conv_local.shape[0]
    lead = taps - 1
    span = extended.shape[1] - lead
    mixed = conv_local[0] * extended[:, lead : lead + span]
    for offset in range(1, taps):
        mixed = mixed + conv_local[offset] * extended[:, lead - offset : lead - offset + span]
    mixed = jax.nn.silu(mixed)
    width = mixed.shape[-1] // 3
    seq_count = mixed.shape[0]
    head_count = width // HEAD_DIM
    block_count = span // BLOCK

    def to_blocks(values):
        shaped = values.reshape(seq_count, block_count, BLOCK, head_count, HEAD_DIM)
        return shaped.transpose(1, 0, 3, 2, 4)

    queries = mixed[..., :width]
    keys = mixed[..., width : 2 * width].reshape(seq_count, span, head_count, HEAD_DIM)
    keys = keys * lax.rsqrt(jnp.sum(keys * keys, -1, keepdims=True) + 1e-06)
    values = mixed[..., 2 * width :]
    betas = jax.nn.sigmoid(logits + bias_local) * live_mask[..., None]
    betas = betas.reshape(seq_count, block_count, BLOCK, head_count).transpose(1, 0, 3, 2)
    return (to_blocks(queries), to_blocks(keys), to_blocks(values), betas)


def finish_heads(outputs, gain_head):
    block_count, seq_count, head_count, size, head_size = outputs.shape
    outputs = outputs.transpose(1, 0, 3, 2, 4).reshape(
        seq_count, block_count * size, head_count, head_size
    )
    normed = outputs * row_scale(outputs) * gain_head
    return normed.reshape(seq_count, block_count * size, head_count * head_size)


def mixer_local(extended, conv_local, logits, bias_local, gain_head, entry, live_mask):
    queries, keys, values, betas = prepare(extended, conv_local, logits, bias_local, live_mask)

    def advance(carried, pieces):
        output, carried = block_advance(carried, pieces[0], pieces[1], pieces[2], pieces[3])
        return (carried, output)

    final, outputs = lax.scan(advance, entry, (queries, keys, values, betas))
    return (finish_heads(outputs, gain_head), final)


def entry_map(entry, stored, gain_head):

    def advance(carried, pieces):
        output, carried = apply_terms(carried, pieces[0], pieces[1], pieces[2], pieces[3])
        return (carried, output)

    final, outputs = lax.scan(advance, entry, stored)
    return (finish_heads(outputs, gain_head), final)


def mixer_links(extended, conv_local, logits, bias_local, live_mask):
    queries, keys, values, betas = prepare(extended, conv_local, logits, bias_local, live_mask)
    state_shape = keys.shape[1:3] + (HEAD_DIM, HEAD_DIM)
    start_pair = (
        jnp.broadcast_to(jnp.eye(HEAD_DIM, dtype=jnp.float32), state_shape),
        jnp.zeros(state_shape, jnp.float32),
    )

    def advance(pair, pieces):
        weighted_keys, weighted_values = block_terms(pieces[0], pieces[1], pieces[2])
        keys_turned = jnp.swapaxes(pieces[0], -1, -2)
        transit = pair[0] - matmul_high(keys_turned, matmul_high(weighted_keys, pair[0]))
        contrib = pair[1] + matmul_high(
            keys_turned, weighted_values - matmul_high(weighted_keys, pair[1])
        )
        return ((transit, contrib), (weighted_keys, weighted_values))

    pair, terms = lax.scan(advance, start_pair, (keys, values, betas))
    return (pair, (queries, keys, terms[0], terms[1]))


def chain_link(earlier, later):
    return (matmul_high(later[0], earlier[0]), matmul_high(later[0], earlier[1]) + later[1])


def spread_rows(values):
    return lax.all_gather(values, "mp", axis=1, tiled=True)


def collect_rows(values):
    return lax.psum_scatter(values, "mp", scatter_dimension=1, tiled=True)


def project(rows, weight):
    return jnp.einsum("bsd,de->bse", rows, weight, preferred_element_type=jnp.float32)


def project_back(grads, weight):
    return jnp.einsum("bse,de->bsd", grads, weight, preferred_element_type=jnp.float32)


def weight_grad(rows, grads):
    return jnp.einsum("bsd,bse->de", rows, grads, preferred_element_type=jnp.float32)


def on_device(
    tokens,
    lengths,
    mixer_gain,
    query_weight,
    key_weight,
    value_weight,
    beta_weight,
    beta_bias,
    conv_weight,
    head_gain,
    out_weight,
    feed_gain,
    gate_weight,
    up_weight,
    down_weight,
    cotangent,
):
    mp_rank = lax.axis_index("mp")
    seq_rank = lax.axis_index("seq")
    local_weights = (
        query_weight,
        key_weight,
        value_weight,
        beta_weight,
        gate_weight,
        up_weight,
        out_weight,
        down_weight,
    )
    gathered = (
        lax.all_gather(local_weights[0], "seq", axis=0, tiled=True),
        lax.all_gather(local_weights[1], "seq", axis=0, tiled=True),
        lax.all_gather(local_weights[2], "seq", axis=0, tiled=True),
        lax.all_gather(local_weights[3], "seq", axis=0, tiled=True),
        lax.all_gather(local_weights[4], "seq", axis=0, tiled=True),
        lax.all_gather(local_weights[5], "seq", axis=0, tiled=True),
        lax.all_gather(local_weights[6], "seq", axis=1, tiled=True),
        lax.all_gather(local_weights[7], "seq", axis=1, tiled=True),
    )
    inputs = tokens.astype(jnp.float32)
    unit_mixer = inputs * row_scale(inputs)
    mixer_rows = spread_rows((unit_mixer * mixer_gain).astype(jnp.bfloat16))
    projected = jnp.concatenate(
        (
            project(mixer_rows, gathered[0]),
            project(mixer_rows, gathered[1]),
            project(mixer_rows, gathered[2]),
        ),
        -1,
    ).astype(jnp.bfloat16)
    logits = project(mixer_rows, gathered[3])
    taps = conv_weight.shape[1]
    lead = taps - 1
    previous = passed_along(projected[:, projected.shape[1] - lead :], "seq", 1)
    extended = jnp.concatenate((previous, projected), 1).astype(jnp.float32)
    local_width = gathered[0].shape[1]
    head_count = local_width // HEAD_DIM
    conv_local = lax.dynamic_slice_in_dim(conv_weight, mp_rank * local_width, local_width, 2)
    conv_local = conv_local.transpose(1, 0, 2).reshape(taps, 3 * local_width)
    bias_local = lax.dynamic_slice_in_dim(beta_bias, mp_rank * head_count, head_count, 0)
    span = mixer_rows.shape[1]
    position = seq_rank * span + jnp.arange(span, dtype=jnp.int32)
    live_mask = (position[None, :] < lengths[:, None]).astype(jnp.float32)
    links, stored = mixer_links(extended, conv_local, logits, bias_local, live_mask)
    identity_pair = (
        jnp.broadcast_to(jnp.eye(HEAD_DIM, dtype=jnp.float32), links[0].shape),
        jnp.zeros_like(links[1]),
    )
    entering = entering_2(links, "seq", chain_link, identity_pair, False)[1]

    def from_entry(entry_in):
        return entry_map(entry_in, stored, head_gain)

    (head_out, leaving), entry_pull = jax.vjp(from_entry, entering)
    norm_total = jnp.sum(jnp.sqrt(jnp.sum(leaving * leaving, (-2, -1))))
    head_rows = head_out.astype(jnp.bfloat16)
    hidden_in = inputs + collect_rows(project(head_rows, gathered[6]))
    unit_feed = hidden_in * row_scale(hidden_in)
    feed_rows = spread_rows((unit_feed * feed_gain).astype(jnp.bfloat16))
    gate_pre = project(feed_rows, gathered[4])
    up_pre = project(feed_rows, gathered[5])
    gate_sig = jax.nn.sigmoid(gate_pre)
    gate_act = gate_pre * gate_sig
    hidden = (gate_act * up_pre).astype(jnp.bfloat16)
    block_output = hidden_in + collect_rows(project(hidden, gathered[7]))
    grad_rows = spread_rows(cotangent)
    grad_hidden = project_back(grad_rows, gathered[7])
    grad_down = weight_grad(hidden, grad_rows)
    grad_gate = (grad_hidden * up_pre * gate_sig * (1.0 + gate_pre * (1.0 - gate_sig))).astype(
        jnp.bfloat16
    )
    grad_up = (grad_hidden * gate_act).astype(jnp.bfloat16)
    grad_feed = collect_rows(
        project_back(grad_gate, gathered[4]) + project_back(grad_up, gathered[5])
    )
    grad_gate_w = weight_grad(feed_rows, grad_gate)
    grad_up_w = weight_grad(feed_rows, grad_up)
    feed_gain_part = jnp.sum(grad_feed * unit_feed, (0, 1))
    grad_hidden_in = cotangent.astype(jnp.float32) + norm_backward(
        grad_feed * feed_gain, unit_feed, row_scale(hidden_in)
    )
    grad_mix_rows = spread_rows(grad_hidden_in.astype(jnp.bfloat16))
    grad_head = project_back(grad_mix_rows, gathered[6])
    grad_out_w = weight_grad(head_rows, grad_mix_rows)
    local_entry = entry_pull((grad_head, jnp.zeros_like(leaving)))[0]
    flipped = (jnp.swapaxes(links[0], -1, -2), local_entry)
    exiting = entering_2(flipped, "seq", chain_link, identity_pair, True)[1]

    def local_mix(ext_in, conv_in, logit_in, bias_in, gain_in, entry_in):
        return mixer_local(ext_in, conv_in, logit_in, bias_in, gain_in, entry_in, live_mask)

    unused, mixer_pull = jax.vjp(
        local_mix, extended, conv_local, logits, bias_local, head_gain, entering
    )
    grads = mixer_pull((grad_head, exiting))
    grad_ext = grads[0]
    returned = passed_along(grad_ext[:, :lead].astype(jnp.bfloat16), "seq", -1).astype(jnp.float32)
    grad_proj = grad_ext[:, lead:]
    grad_proj = grad_proj.at[:, span - lead :].add(returned).astype(jnp.bfloat16)
    grad_logit = grads[2].astype(jnp.bfloat16)
    grad_query = grad_proj[..., :local_width]
    grad_key = grad_proj[..., local_width : 2 * local_width]
    grad_value = grad_proj[..., 2 * local_width :]
    grad_mixer = collect_rows(
        project_back(grad_query, gathered[0])
        + project_back(grad_key, gathered[1])
        + project_back(grad_value, gathered[2])
        + project_back(grad_logit, gathered[3])
    )
    grad_query_w = weight_grad(mixer_rows, grad_query)
    grad_key_w = weight_grad(mixer_rows, grad_key)
    grad_value_w = weight_grad(mixer_rows, grad_value)
    grad_beta_w = weight_grad(mixer_rows, grad_logit)
    mixer_gain_part = jnp.sum(grad_mixer * unit_mixer, (0, 1))
    tokens_grad = grad_hidden_in + norm_backward(
        grad_mixer * mixer_gain, unit_mixer, row_scale(inputs)
    )
    weight_parts = (
        grad_query_w,
        grad_key_w,
        grad_value_w,
        grad_beta_w,
        grad_gate_w,
        grad_up_w,
        grad_out_w,
        grad_down,
    )
    shared = (
        lax.psum_scatter(weight_parts[0], "seq", scatter_dimension=0, tiled=True),
        lax.psum_scatter(weight_parts[1], "seq", scatter_dimension=0, tiled=True),
        lax.psum_scatter(weight_parts[2], "seq", scatter_dimension=0, tiled=True),
        lax.psum_scatter(weight_parts[3], "seq", scatter_dimension=0, tiled=True),
        lax.psum_scatter(weight_parts[4], "seq", scatter_dimension=0, tiled=True),
        lax.psum_scatter(weight_parts[5], "seq", scatter_dimension=0, tiled=True),
        lax.psum_scatter(weight_parts[6], "seq", scatter_dimension=1, tiled=True),
        lax.psum_scatter(weight_parts[7], "seq", scatter_dimension=1, tiled=True),
    )
    conv_grad = grads[1].reshape(taps, 3, local_width).transpose(1, 0, 2)
    conv_full = lax.dynamic_update_slice_in_dim(
        jnp.zeros(conv_weight.shape, jnp.float32), conv_grad, mp_rank * local_width, 2
    )
    bias_full = lax.dynamic_update_slice_in_dim(
        jnp.zeros(beta_bias.shape, jnp.float32), grads[3], mp_rank * head_count, 0
    )
    totals = lax.psum(
        (mixer_gain_part, feed_gain_part, grads[4], bias_full, conv_full, norm_total), ("seq", "mp")
    )
    state_norm = totals[5] / (NSEQ * HEADS * lax.axis_size("seq"))
    return (
        block_output,
        tokens_grad,
        totals[0],
        shared[0],
        shared[1],
        shared[2],
        shared[3],
        totals[3],
        totals[4],
        totals[2],
        shared[6],
        totals[1],
        shared[4],
        shared[5],
        shared[7],
        state_norm,
    )


def solution(mesh):
    placed = (
        P(None, ("seq", "mp"), None),
        P(),
        P(),
        P("seq", "mp"),
        P("seq", "mp"),
        P("seq", "mp"),
        P("seq", "mp"),
        P(),
        P(),
        P(),
        P("mp", "seq"),
        P(),
        P("seq", "mp"),
        P("seq", "mp"),
        P("mp", "seq"),
        P(None, ("seq", "mp"), None),
    )
    return jax.shard_map(
        on_device,
        mesh=mesh,
        in_specs=placed,
        out_specs=(
            P(None, ("seq", "mp"), None),
            P(None, ("seq", "mp"), None),
            P(),
            P("seq", "mp"),
            P("seq", "mp"),
            P("seq", "mp"),
            P("seq", "mp"),
            P(),
            P(),
            P(),
            P("mp", "seq"),
            P(),
            P("seq", "mp"),
            P("seq", "mp"),
            P("mp", "seq"),
            P(),
        ),
        check_vma=False,
    )
```

profile of v0, /device:TPU:0, one launch (start us, length us, event | category | flops | bytes accessed | tf_op | source)
XLA Modules:
  0.0 2029.3 jit_solution(6172161053373182506)
XLA Ops:
  24.2 35.1 %all-gather.20.cloned.1.call-done = bf16[2,256,2048]{2,1,0:T(8,128)(2,1)} async-done(((bf16[2,64,2048]{2,1,0:T(8,128)(2,1)}), bf16[2,256,2048]{2,1,0:T(8,128)(2,1)}) %all-gather.20.cloned.1.call-update) | async-done | bytes 2097168 | tf_op jit(solution)/shard_map/all_gather | solution.py:163
  171.8 44.8 %while.177 = (s32[]{:T(128)}, f32[2,4,128,128]{3,2,1,0:T(8,128)S(1)}, f32[2,4,128,128]{3,2,1,0:T(8,128)S(1)}, f32[4,2,4,64,128]{4,3,2,1,0:T(8,128)}, f32[4,2,4,6...) while((s32[]{:T(128)}, ...), condition=%wide.region_3.4_spmd.clone, body=%wide.region_2.3_spmd.clone.sunk | while | flops 806301760 | bytes 11268736 | solution.py:154
  223.0 33.7 %all-gather.42.cloned.1.call-done = f32[16,4,128,128]{3,2,1,0:T(8,128)} async-done(((f32[2,4,128,128]{3,2,1,0:T(8,128)}), f32[16,4,128,128]{3,2,1,0:T(8,128)}) %all-gather.42.cloned.1.call-update) | async-done | bytes 4194320 | tf_op jit(solution)/shard_map/all_gather | solution.py:24
  256.7 39.1 %all-gather.44.cloned.1.call-done = f32[16,4,128,128]{3,2,1,0:T(8,128)} async-done(((f32[2,4,128,128]{3,2,1,0:T(8,128)}), f32[16,4,128,128]{3,2,1,0:T(8,128)}) %all-gather.44.cloned.1.call-update) | async-done | bytes 4194320 | tf_op jit(solution)/shard_map/all_gather | solution.py:24
  361.3 74.8 %reduce-scatter.15.cloned.1.call-done = f32[2,64,2048]{2,1,0:T(8,128)} async-done(((f32[2,256,2048]{2,1,0:T(8,128)}), f32[2,64,2048]{2,1,0:T(8,128)}) %reduce-scatter.15.cloned.1.call-update) | async-done | bytes 1048592 | tf_op jit(solution)/shard_map/reduce_scatter | solution.py:167
  440.8 43.5 %all-gather.38.cloned.1.call-done = bf16[2,256,2048]{2,1,0:T(8,128)(2,1)} async-done(((bf16[2,64,2048]{2,1,0:T(8,128)(2,1)}), bf16[2,256,2048]{2,1,0:T(8,128)(2,1)}) %all-gather.38.cloned.1.call-update) | async-done | bytes 2097168 | tf_op jit(solution)/shard_map/all_gather | solution.py:163
  484.3 45.0 %all-gather.36.cloned.1.call-done = bf16[1408,2048]{1,0:T(8,128)(2,1)} async-done(((bf16[1408,256]{1,0:T(8,128)(2,1)}), bf16[1408,2048]{1,0:T(8,128)(2,1)}) %all-gather.36.cloned.1.call-update) | async-done | bytes 5767184 | tf_op jit(solution)/shard_map/all_gather | solution.py:220
  537.7 37.1 %all-gather.34.cloned.1.call-done = bf16[2048,1408]{1,0:T(8,128)(2,1)} async-done(((bf16[256,1408]{1,0:T(8,128)(2,1)}), bf16[2048,1408]{1,0:T(8,128)(2,1)}) %all-gather.34.cloned.1.call-update) | async-done | bytes 5767184 | tf_op jit(solution)/shard_map/all_gather | solution.py:218
  574.7 48.1 %all-gather.30.cloned.1.call-done = bf16[2,256,2048]{2,1,0:T(8,128)(2,1)} async-done(((bf16[2,64,2048]{2,1,0:T(8,128)(2,1)}), bf16[2,256,2048]{2,1,0:T(8,128)(2,1)}) %all-gather.30.cloned.1.call-update) | async-done | bytes 2097168 | tf_op jit(solution)/shard_map/all_gather | solution.py:163
  631.0 35.9 %all-gather.32.cloned.1.call-done = bf16[2048,1408]{1,0:T(8,128)(2,1)} async-done(((bf16[256,1408]{1,0:T(8,128)(2,1)}), bf16[2048,1408]{1,0:T(8,128)(2,1)}) %all-gather.32.cloned.1.call-update) | async-done | bytes 5767184 | tf_op jit(solution)/shard_map/all_gather | solution.py:217
  686.5 76.7 %reduce-scatter.19.cloned.1.call-done = f32[2,64,2048]{2,1,0:T(8,128)} async-done(((f32[2,256,2048]{2,1,0:T(8,128)}), f32[2,64,2048]{2,1,0:T(8,128)}) %reduce-scatter.19.cloned.1.call-update) | async-done | bytes 1048592 | tf_op jit(solution)/shard_map/reduce_scatter | solution.py:167
  796.3 87.8 %while.176 = (s32[]{:T(128)}, f32[2,4,128,128]{3,2,1,0:T(8,128)S(1)}, f32[4,2,4,64,128]{4,3,2,1,0:T(8,128)}, f32[4,2,4,64,1]{3,2,1,4,0:T(4,128)S(1)}, f32[4,2,4,...) while((s32[]{:T(128)}, ...), condition=%wide.region_20.21_spmd.clone.clone, body=%wide.region_19.20_spmd.clone.clone.sunk | while | flops 806428672 | bytes 25407840 | solution.py:123
  982.5 175.4 %while.175 = (s32[]{:T(128)}, f32[2,4,128,128]{3,2,1,0:T(8,128)S(1)}, f32[4,2,4,64,128]{4,3,2,1,0:T(8,128)}, f32[4,2,4,64,128]{4,3,2,1,0:T(8,128)}, f32[4,2,4,64...) while((s32[]{:T(128)}, ...), condition=%wide.region_27.28_spmd.clone, body=%wide.region_23.27_spmd.clone.sunk | while | flops 1612381696 | bytes 52625072 | solution.py:123
  1281.0 34.8 %reduce-scatter.21.cloned.1.call-done = f32[2,64,2048]{2,1,0:T(8,128)} async-done(((f32[2,256,2048]{2,1,0:T(8,128)}), f32[2,64,2048]{2,1,0:T(8,128)}) %reduce-scatter.21.cloned.1.call-update) | async-done | bytes 1048592 | tf_op jit(solution)/shard_map/reduce_scatter | solution.py:167
  1317.4 43.6 %all-reduce.11 = (f32[2048]{0:T(1024)}, f32[16]{0:T(128)}, f32[128]{0:T(128)}, f32[2048]{0:T(1024)}, f32[]{:T(128)}) all-reduce(f32[2048]{0:T(1024)S(1)} %get-tuple-element.2489, f32[16]{0:T(128)S(1)} %dynamic_update_slice.261, f32[128]{0:T(128)S(1)} %bitcast_reduce_fusion, ...), channel_id=1, replica_groups=mesh['seq'=8,'mp'=4] {'seq','mp'}, use_global_device_ids=true, to_apply=%region_32.33 | all-reduce | flops 4241 | bytes 33928 | tf_op jit(solution)/shard_map/psum | solution.py:347
  1361.7 34.7 %reduce-scatter.17.cloned.1.call-done = f32[2,64,2048]{2,1,0:T(8,128)} async-done(((f32[2,256,2048]{2,1,0:T(8,128)}), f32[2,64,2048]{2,1,0:T(8,128)}) %reduce-scatter.17.cloned.1.call-update) | async-done | bytes 1048592 | tf_op jit(solution)/shard_map/reduce_scatter | solution.py:167
  1400.0 87.7 %reduce-scatter.31.cloned.1.call-done = f32[256,1408]{1,0:T(8,128)} async-done(((f32[2048,1408]{1,0:T(8,128)}), f32[256,1408]{1,0:T(8,128)}) %reduce-scatter.31.cloned.1.call-update) | async-done | bytes 1441808 | tf_op jit(solution)/shard_map/reduce_scatter | solution.py:335
  1487.8 90.9 %reduce-scatter.33.cloned.1.call-done = f32[256,1408]{1,0:T(8,128)} async-done(((f32[2048,1408]{1,0:T(8,128)}), f32[256,1408]{1,0:T(8,128)}) %reduce-scatter.33.cloned.1.call-update) | async-done | bytes 1441808 | tf_op jit(solution)/shard_map/reduce_scatter | solution.py:336
  1578.6 90.9 %reduce-scatter.35.cloned.1.call-done = f32[1408,256]{1,0:T(8,128)} async-done(((f32[1408,2048]{1,0:T(8,128)}), f32[1408,256]{1,0:T(8,128)}) %reduce-scatter.35.cloned.1.call-update) | async-done | bytes 1441808 | tf_op jit(solution)/shard_map/reduce_scatter | solution.py:338
  1669.5 55.1 %reduce-scatter.29.cloned.1.call-done = f32[512,256]{1,0:T(8,128)} async-done(((f32[512,2048]{1,0:T(8,128)}), f32[512,256]{1,0:T(8,128)}) %reduce-scatter.29.cloned.1.call-update) | async-done | bytes 524304 | tf_op jit(solution)/shard_map/reduce_scatter | solution.py:337
  1724.7 127.6 %all-reduce.14.cloned.1.call-done = f32[3,4,2048]{2,1,0:T(4,128)} async-done(((f32[3,4,2048]{2,1,0:T(4,128)}), f32[3,4,2048]{2,1,0:T(4,128)}) %all-reduce.14.cloned.1.call-update) | async-done | bytes 98320 | tf_op jit(solution)/shard_map/psum | solution.py:347
  1852.3 56.4 %reduce-scatter.23.cloned.1.call-done = f32[256,512]{1,0:T(8,128)} async-done(((f32[2048,512]{1,0:T(8,128)}), f32[256,512]{1,0:T(8,128)}) %reduce-scatter.23.cloned.1.call-update) | async-done | bytes 524304 | tf_op jit(solution)/shard_map/reduce_scatter | solution.py:331
  1908.7 55.1 %reduce-scatter.25.cloned.1.call-done = f32[256,512]{1,0:T(8,128)} async-done(((f32[2048,512]{1,0:T(8,128)}), f32[256,512]{1,0:T(8,128)}) %reduce-scatter.25.cloned.1.call-update) | async-done | bytes 524304 | tf_op jit(solution)/shard_map/reduce_scatter | solution.py:332
  1963.8 55.7 %reduce-scatter.27.cloned.1.call-done = f32[256,512]{1,0:T(8,128)} async-done(((f32[2048,512]{1,0:T(8,128)}), f32[256,512]{1,0:T(8,128)}) %reduce-scatter.27.cloned.1.call-update) | async-done | bytes 524304 | tf_op jit(solution)/shard_map/reduce_scatter | solution.py:333
  (848 shorter events, 891.8 us)
Async XLA Ops:
  12.0 135.3 %all-gather.26.cloned.1.call-start = ((), (), s32[]{:S(2)}) async-start(), calls=%async_computation.15 | async-start | bytes 2359296 | tf_op jit(solution)/shard_map/all_gather | solution.py:215
  12.6 244.1 %all-gather.42.cloned.1.call-start = ((), (), s32[]{:S(2)}) async-start(), calls=%async_computation.35 | async-start | bytes 4718592 | tf_op jit(solution)/shard_map/all_gather | solution.py:24
  218.0 135.6 %all-gather.28.cloned.1.call-start = ((), (), s32[]{:S(2)}) async-start(), calls=%async_computation.16 | async-start | bytes 2359296 | tf_op jit(solution)/shard_map/all_gather | solution.py:219
  218.8 217.4 %reduce-scatter.15.cloned.1.call-start = ((), (), s32[]{:S(2)}) async-start(), calls=%async_computation.17 | async-start | bytes 5242880 | tf_op jit(solution)/shard_map/reduce_scatter | solution.py:167
  359.2 125.1 %all-gather.38.cloned.1.call-start = ((), (), s32[]{:S(2)}) async-start(), calls=%async_computation.23 | async-start | bytes 2621440 | tf_op jit(solution)/shard_map/all_gather | solution.py:163
  360.0 169.3 %all-gather.36.cloned.1.call-start = ((), (), s32[]{:S(2)}) async-start(), calls=%async_computation.21 | async-start | bytes 6488064 | tf_op jit(solution)/shard_map/all_gather | solution.py:220
  360.6 214.1 %all-gather.34.cloned.1.call-start = ((), (), s32[]{:S(2)}) async-start(), calls=%async_computation.20 | async-start | bytes 6488064 | tf_op jit(solution)/shard_map/all_gather | solution.py:218
  361.3 261.5 %all-gather.30.cloned.1.call-start = ((), (), s32[]{:S(2)}) async-start(), calls=%async_computation.18 | async-start | bytes 2621440 | tf_op jit(solution)/shard_map/all_gather | solution.py:163
  439.6 227.3 %all-gather.32.cloned.1.call-start = ((), (), s32[]{:S(2)}) async-start(), calls=%async_computation.19 | async-start | bytes 6488064 | tf_op jit(solution)/shard_map/all_gather | solution.py:217
  440.3 322.9 %reduce-scatter.19.cloned.1.call-start = ((), (), s32[]{:S(2)}) async-start(), calls=%async_computation.24 | async-start | bytes 5242880 | tf_op jit(solution)/shard_map/reduce_scatter | solution.py:167
  686.3 197.8 %all-gather.40.cloned.1.call-start = ((), (), s32[]{:S(2)}) async-start(), calls=%async_computation.25 | async-start | bytes 2621440 | tf_op jit(solution)/shard_map/all_gather | solution.py:163
  768.5 162.1 %all-gather.46.cloned.1.call-start = ((), (), s32[]{:S(2)}) async-start(), calls=%async_computation.37 | async-start | bytes 4718592 | tf_op jit(solution)/shard_map/all_gather | solution.py:24
  769.6 194.0 %all-gather.48.cloned.1.call-start = ((), (), s32[]{:S(2)}) async-start(), calls=%async_computation.38 | async-start | bytes 4718592 | tf_op jit(solution)/shard_map/all_gather | solution.py:24
  926.2 353.2 %reduce-scatter.37.cloned.1.call-start = ((), (), s32[]{:S(2)}) async-start(), calls=%async_computation.39 | async-start | bytes 1179648
  1198.6 117.2 %reduce-scatter.21.cloned.1.call-start = ((), (), s32[]{:S(2)}) async-start(), calls=%async_computation.26 | async-start | bytes 5242880 | tf_op jit(solution)/shard_map/reduce_scatter | solution.py:167
  1210.1 186.3 %reduce-scatter.17.cloned.1.call-start = ((), (), s32[]{:S(2)}) async-start(), calls=%async_computation.22 | async-start | bytes 5242880 | tf_op jit(solution)/shard_map/reduce_scatter | solution.py:167
  1218.8 269.0 %reduce-scatter.31.cloned.1.call-start = ((), (), s32[]{:S(2)}) async-start(), calls=%async_computation.32 | async-start | bytes 12976128 | tf_op jit(solution)/shard_map/reduce_scatter | solution.py:335
  1228.5 350.1 %reduce-scatter.33.cloned.1.call-start = ((), (), s32[]{:S(2)}) async-start(), calls=%async_computation.33 | async-start | bytes 12976128 | tf_op jit(solution)/shard_map/reduce_scatter | solution.py:336
  1238.4 431.2 %reduce-scatter.35.cloned.1.call-start = ((), (), s32[]{:S(2)}) async-start(), calls=%async_computation.34 | async-start | bytes 12976128 | tf_op jit(solution)/shard_map/reduce_scatter | solution.py:338
  1248.3 476.4 %reduce-scatter.29.cloned.1.call-start = ((), (), s32[]{:S(2)}) async-start(), calls=%async_computation.31 | async-start | bytes 4718592 | tf_op jit(solution)/shard_map/reduce_scatter | solution.py:337
  1254.2 598.1 %all-reduce.14.cloned.1.call-start = ((), (), s32[]{:S(2)}) async-start(), calls=%async_computation.30 | async-start | bytes 196608 | tf_op jit(solution)/shard_map/psum | solution.py:347
  1255.0 653.7 %reduce-scatter.23.cloned.1.call-start = ((), (), s32[]{:S(2)}) async-start(), calls=%async_computation.27 | async-start | bytes 4718592 | tf_op jit(solution)/shard_map/reduce_scatter | solution.py:331
  1259.4 704.4 %reduce-scatter.25.cloned.1.call-start = ((), (), s32[]{:S(2)}) async-start(), calls=%async_computation.28 | async-start | bytes 4718592 | tf_op jit(solution)/shard_map/reduce_scatter | solution.py:332
  1263.8 755.7 %reduce-scatter.27.cloned.1.call-start = ((), (), s32[]{:S(2)}) async-start(), calls=%async_computation.29 | async-start | bytes 4718592 | tf_op jit(solution)/shard_map/reduce_scatter | solution.py:333
  (106 other events, 3642.5 us)
Sparse Core Ops, SparseCore 0:
  10.7 48.6 all-gather.19
  217.6 39.1 all-gather.41
  259.0 36.7 all-gather.43
  359.3 76.7 reduce-scatter.14
  437.8 46.4 all-gather.37
  486.2 43.0 all-gather.35
  531.4 43.3 all-gather.33
  576.8 45.9 all-gather.29
  624.8 42.0 all-gather.31
  686.4 76.7 reduce-scatter.18
  768.6 46.4 all-gather.39
  817.5 35.4 all-gather.45
  926.3 37.2 all-gather.47
  1198.7 37.9 reduce-scatter.36
  1239.0 76.7 reduce-scatter.20
  1318.0 78.3 reduce-scatter.16
  1400.5 87.2 reduce-scatter.30
  1491.8 86.7 reduce-scatter.32
  1582.7 86.7 reduce-scatter.34
  1673.3 51.3 reduce-scatter.28
  1731.8 120.4 all-reduce.13
  1856.5 52.1 reduce-scatter.22
  1912.5 51.2 reduce-scatter.24
  1968.1 51.3 reduce-scatter.26
  (4 shorter events, 110.3 us)
where the time goes:
time: 2040 us; the launch traced here: 2030 us
  waiting for transfers between devices  1280 us (63%)
  matrix products  493 us (24%)
  local copies, waits for them, and re-layouts  119 us (6%)
  other arithmetic  57.5 us (3%)
  blocking collectives  54.1 us (3%)
    dot_general x304, matrix products, matmul_high(): return jnp.matmul(left, right, precision=HIGHEST)  342 us
    reduce_scatter x4, waiting for transfers between devices, collect_rows(): return lax.psum_scatter(values, 'mp', scatter_dimension=1, tiled=True)  221 us
    psum x1, waiting for transfers between devices, on_device(): lax.psum((mixer_gain_part, feed_gain_part, grads[4], bias_full, conv_full...  128 us
    all_gather x4, waiting for transfers between devices, spread_rows(): return lax.all_gather(values, 'mp', axis=1, tiled=True)  127 us
    all_gather x4, waiting for transfers between devices, entering_2(): everything = jax.tree.map(lambda part: lax.all_gather(part, axis), x)  106 us
    reduce_scatter x1, waiting for transfers between devices, on_device(): lax.psum_scatter(weight_parts[7], 'seq', scatter_dimension=1, tiled=True)  90.9 us
    reduce_scatter x1, waiting for transfers between devices, on_device(): lax.psum_scatter(weight_parts[5], 'seq', scatter_dimension=0, tiled=True)  90.9 us
    reduce_scatter x1, waiting for transfers between devices, on_device(): lax.psum_scatter(weight_parts[4], 'seq', scatter_dimension=0, tiled=True)  87.7 us
  transfers between devices with their start and end apart: 30, of which 24 were waited for; matrix products, arithmetic and copies ran while one was open for 17% of the time, Pallas kernels for 0%

commit v1 on v0

v1 whole, which is shorter than its diff:
```python
import functools

import jax
import jax.numpy as jnp
from jax import lax
from jax.experimental import pallas as pl
from jax.experimental.pallas import tpu as pltpu
from jax.sharding import PartitionSpec as P

HEADS = 16
HEAD_DIM = 128
NSEQ = 2
EPSILON = 1e-05
KEY_EPSILON = 1e-06
LANES = 128
LEAD = 8
EDGE = 16
BF = jnp.bfloat16
F32 = jnp.float32
MESH = pl.DeviceIdType.MESH
VMEM = pl.BlockSpec(memory_space=pltpu.VMEM)
SMEM = pl.BlockSpec(memory_space=pltpu.SMEM)
ANY = pl.BlockSpec(memory_space=pl.ANY)
NN = (((1,), (0,)), ((), ()))
NT = (((1,), (1,)), ((), ()))
TN = (((0,), (0,)), ((), ()))
DMA = pltpu.SemaphoreType.DMA


def dot(left, right, dims=NN):
    return lax.dot_general(left, right, dims, preferred_element_type=F32)


def halves(values):
    high = values.astype(BF)
    return high, (values - high.astype(F32)).astype(BF)


def fine(left, right, dims=NN):
    return (
        dot(left[0], right[0], dims)
        + dot(left[0], right[1], dims)
        + dot(left[1], right[0], dims)
    )


def row_scale(values):
    return lax.rsqrt(jnp.mean(values * values, -1, keepdims=True) + EPSILON)


def norm_backward(grad_normed, unit_rows, scale):
    return scale * (grad_normed - unit_rows * jnp.mean(grad_normed * unit_rows, -1, keepdims=True))


def sigmoid(values):
    return 1.0 / (1.0 + jnp.exp(-values))


def iota(shape, dim):
    return lax.broadcasted_iota(jnp.int32, shape, dim)


def lower_mask(size, strict):
    rows, cols = iota((size, size), 0), iota((size, size), 1)
    return rows > cols if strict else rows >= cols


def unit_lower_inverses(lowers):
    size = LANES
    rows, cols = iota((size, size), 0), iota((size, size), 1)
    eye = (rows == cols).astype(F32)
    blocks = [low[at : at + size, at : at + size] for low in lowers for at in (0, size)]
    base = 16
    same = (rows // base) == (cols // base)
    minus = [jnp.where(same, -block, 0.0) for block in blocks]
    inverses = [eye + one for one in minus]
    pairs = [halves(one) for one in minus]
    powers = [fine(pair, pair) for pair in pairs]
    covered = 2
    while covered * 2 < base:
        lefts = [halves(jnp.concatenate((i, p), 0)) for i, p in zip(inverses, powers)]
        both = [fine(left, (left[0][size:], left[1][size:])) for left in lefts]
        inverses = [i + b[:size] for i, b in zip(inverses, both)]
        powers = [b[size:] for b in both]
        covered *= 2
    inverses = [i + fine(halves(i), halves(p)) for i, p in zip(inverses, powers)]
    while base < size:
        joined = (rows // (2 * base)) == (cols // (2 * base))
        cross = jnp.logical_and(joined, jnp.logical_not(same))
        pairs = [halves(i) for i in inverses]
        inner = [fine(halves(jnp.where(cross, b, 0.0)), i) for b, i in zip(blocks, pairs)]
        inverses = [i - fine(p, halves(x)) for i, p, x in zip(inverses, pairs, inner)]
        same = joined
        base *= 2
    pairs = [halves(i) for i in inverses]
    corners = [fine(halves(low[size:, :size]), pairs[2 * k]) for k, low in enumerate(lowers)]
    corners = [-fine(pairs[2 * k + 1], halves(c)) for k, c in enumerate(corners)]
    zero = jnp.zeros((size, size), F32)
    return [
        jnp.concatenate(
            (
                jnp.concatenate((inverses[2 * k], zero), 1),
                jnp.concatenate((corner, inverses[2 * k + 1]), 1),
            ),
            0,
        )
        for k, corner in enumerate(corners)
    ]


def flip(index, mask):
    out = index
    bit = 1
    while bit <= mask:
        if mask & bit:
            out = out + bit * (1 - 2 * ((index // bit) % 2))
        bit *= 2
    return out


def bits_of(count):
    out = []
    bit = 1
    while bit < count:
        out.insert(0, bit)
        bit *= 2
    return out


def two_orders(bits):
    if len(bits) < 2:
        return (bits, bits)
    return (list(bits), [bits[1], bits[0]] + list(bits[2:]))


def spans(bits):
    masks = [0]
    for bit in bits:
        masks = masks + [mask ^ bit for mask in masks]
    return masks


def remote(src, dst, send, recv, target):
    return pltpu.make_async_remote_copy(
        src_ref=src,
        dst_ref=dst,
        send_sem=send,
        recv_sem=recv,
        device_id=target,
        device_id_type=MESH,
    )


def greet(targets):
    barrier = pltpu.get_barrier_semaphore()
    for target in targets:
        pl.semaphore_signal(barrier, inc=1, device_id=target, device_id_type=MESH)


def await_all(targets):
    pl.semaphore_wait(pltpu.get_barrier_semaphore(), len(targets))


def meet(targets):
    greet(targets)
    await_all(targets)


def line_mates(geo):
    s, m = geo.s, geo.m
    return [(s, (m + 1) % geo.nm), (s, (m + geo.nm - 1) % geo.nm)]


def cube_mates(geo):
    return [(flip(geo.s, bit), geo.m) for bit in bits_of(geo.ns)]


def all_mates(geo):
    return [((geo.s + k) % geo.ns, geo.m) for k in range(1, geo.ns)]


class Geo:
    def __init__(self, sizes):
        self.ns, self.nm = sizes
        self.s = lax.axis_index("seq")
        self.m = lax.axis_index("mp")


class CubeGather:
    @staticmethod
    def sems(ns):
        return [DMA((2, ns - 1)), DMA((2, ns - 1)), DMA(())]

    def __init__(self, geo, shard, full, sems):
        self.geo, self.shard, self.full = geo, shard, full
        self.send, self.recv, self.local = sems
        self.rows = shard.shape[0]
        self.orders = two_orders(bits_of(geo.ns))
        self.ids = {}
        for order, bits in enumerate(self.orders):
            count = 0
            for step in range(len(bits)):
                for mask in spans(bits[:step]):
                    self.ids[order, step, mask] = count
                    count += 1
        self.todo = sorted(self.ids, key=lambda key: (key[1], bin(key[2]).count("1"), key[2], key[0]))
        self.started = []

    def block(self, order, mask):
        half = self.rows // 2
        start = flip(self.geo.s, mask) * self.rows + order * half
        return self.full.at[pl.ds(pl.multiple_of(start, half), half)]

    def copy(self, order, step, mask, incoming=False):
        bit = self.orders[order][step]
        half = self.rows // 2
        place = self.block(order, mask ^ bit if incoming else mask)
        src = self.shard.at[pl.ds(order * half, half)] if mask == 0 and not incoming else place
        at = self.ids[order, step, mask]
        return remote(
            src, place, self.send.at[order, at], self.recv.at[order, at],
            (flip(self.geo.s, bit), self.geo.m),
        )

    def own(self):
        start = pl.multiple_of(self.geo.s * self.rows, self.rows)
        return pltpu.make_async_copy(self.shard, self.full.at[pl.ds(start, self.rows)], self.local)

    def begin(self, steps=None):
        depth = len(self.orders[0])
        for step in range(depth) if steps is None else steps:
            for order in range(2):
                self.copy(order, step, 0).start()
            if step == depth - 1:
                self.own().start()

    def advance(self, count=None):
        count = len(self.todo) if count is None else count
        for order, step, mask in self.todo[:count]:
            self.copy(order, step, mask, incoming=True).wait_recv()
            after = mask ^ self.orders[order][step]
            for later in range(step + 1, len(self.orders[order])):
                self.copy(order, later, after).start()
        self.todo = self.todo[count:]

    def settle(self):
        self.advance()
        self.own().wait()

    def finish(self):
        for order, step, mask in self.ids:
            self.copy(order, step, mask).wait_send()


class CubeScatter:
    @staticmethod
    def scratch(ns, rows, cols):
        return [pltpu.VMEM((2, ns - 1, rows // 2, cols), BF), DMA((2, ns - 1)), DMA((2, ns - 1))]

    def __init__(self, geo, total, scratch):
        self.geo, self.total = geo, total
        self.slots, self.send, self.recv = scratch
        self.half = self.slots.shape[2]
        self.orders = [list(reversed(bits)) for bits in two_orders(bits_of(geo.ns))]
        self.ids = {}
        for order, bits in enumerate(self.orders):
            count = 0
            for step in range(len(bits)):
                for mask in reversed(spans(bits[step + 1 :])):
                    self.ids[order, step, mask] = count
                    count += 1
        depth = len(self.orders[0])

        def urgency(key):
            order, step, mask = key
            ahead = [k for k in range(depth) if mask & self.orders[order][k]]
            return (step, ahead[0] if ahead else depth, -mask, order)

        self.todo = sorted(self.ids, key=urgency)

    def rows(self, order, mask):
        start = flip(self.geo.s, mask) * (2 * self.half) + order * self.half
        return pl.ds(pl.multiple_of(start, self.half), self.half)

    def copy(self, order, step, mask):
        bit = self.orders[order][step]
        at = self.ids[order, step, mask]
        return remote(
            self.total.at[self.rows(order, mask ^ bit)], self.slots.at[order, at],
            self.send.at[order, at], self.recv.at[order, at],
            (flip(self.geo.s, bit), self.geo.m),
        )

    def begin(self):
        for order, step, mask in self.todo:
            if step == 0:
                self.copy(order, 0, mask).start()

    def advance(self, count=None):
        count = len(self.todo) if count is None else count
        for order, step, mask in self.todo[:count]:
            self.copy(order, step, mask).wait_recv()
            if mask == 0 and step == len(self.orders[order]) - 1:
                continue
            rows = self.rows(order, mask)
            slot = self.slots[order, self.ids[order, step, mask]]
            self.total[rows, :] = (self.total[rows, :].astype(F32) + slot.astype(F32)).astype(BF)
            bits = self.orders[order]
            if step + 1 < len(bits) and mask & bits[step + 1]:
                self.copy(order, step + 1, mask ^ bits[step + 1]).start()
        self.todo = self.todo[count:]

    def finish(self, out):
        self.advance()
        for order in range(2):
            last = self.ids[order, len(self.orders[order]) - 1, 0]
            out[pl.ds(order * self.half, self.half), :] = self.total[self.rows(order, 0), :].astype(
                F32
            ) + self.slots[order, last].astype(F32)
        for order, step, mask in self.ids:
            self.copy(order, step, mask).wait_send()


class LineGather:
    @staticmethod
    def sems(nm):
        return [DMA((2, NSEQ, nm - 1)), DMA((2, NSEQ, nm - 1))]

    def __init__(self, geo, full, sems):
        self.geo, self.full = geo, full
        self.send, self.recv = sems
        self.span = full.shape[1] // geo.nm

    def place(self, piece, origin):
        return self.full.at[piece, pl.ds(pl.multiple_of(origin * self.span, self.span), self.span)]

    def copy(self, way, piece, hop, incoming=False):
        m = self.geo.m
        sign = 1 if way == 0 else -1
        origin = m - sign * (hop + (1 if incoming else 0))
        place = self.place(piece, origin)
        return remote(
            place, place, self.send.at[way, piece, hop], self.recv.at[way, piece, hop],
            (self.geo.s, m + sign),
        )

    def sends(self, way, hop):
        m, nm = self.geo.m, self.geo.nm
        if way == 0:
            return jnp.logical_and(m >= hop, m < nm - 1)
        return jnp.logical_and(m <= nm - 1 - hop, m > 0)

    def receives(self, way, hop):
        m, nm = self.geo.m, self.geo.nm
        return m >= hop + 1 if way == 0 else m <= nm - 2 - hop

    def begin(self, piece):
        for way in range(2):
            @pl.when(self.sends(way, 0))
            def _(way=way):
                self.copy(way, piece, 0).start()

    def advance(self, piece, hop):
        for way in range(2):
            @pl.when(self.receives(way, hop))
            def _(way=way):
                self.copy(way, piece, hop, incoming=True).wait_recv()

            if hop + 1 < self.geo.nm - 1:
                @pl.when(self.sends(way, hop + 1))
                def _(way=way):
                    self.copy(way, piece, hop + 1).start()

    def finish(self, piece):
        for way in range(2):
            for hop in range(self.geo.nm - 1):
                @pl.when(self.sends(way, hop))
                def _(way=way, hop=hop):
                    self.copy(way, piece, hop).wait_send()


class LineScatter:
    @staticmethod
    def scratch(nm, span, cols):
        return [
            pltpu.VMEM((2, NSEQ, nm, span, cols), BF),
            DMA((2, NSEQ, nm)),
            DMA((2, NSEQ, nm)),
        ]

    def __init__(self, geo, part, scratch):
        self.geo, self.part = geo, part
        self.slots, self.send, self.recv = scratch
        self.span = self.slots.shape[3]

    def place(self, way):
        return self.geo.m if way == 0 else self.geo.nm - 1 - self.geo.m

    def own(self, way, piece, block):
        at = self.geo.nm - 1 - block if way == 0 else block
        start = at * self.span
        if not isinstance(start, int):
            start = pl.multiple_of(start, self.span)
        return self.part.at[piece, pl.ds(start, self.span)]

    def copy(self, way, piece, block, first=False):
        slot = self.slots.at[way, piece, block]
        src = self.own(way, piece, block) if first else slot
        step = 1 if way == 0 else -1
        return remote(
            src, slot, self.send.at[way, piece, block], self.recv.at[way, piece, block],
            (self.geo.s, self.geo.m + step),
        )

    def begin(self, piece):
        for way in range(2):
            @pl.when(self.place(way) == 0)
            def _(way=way):
                self.copy(way, piece, 0, True).start()

    def advance(self, piece, turn):
        forward = turn <= self.geo.nm - 2
        for way in range(2):
            at = self.place(way)
            if forward:
                @pl.when(at == 0)
                def _(way=way):
                    self.copy(way, piece, turn - 1, True).wait_send()
                    self.copy(way, piece, turn, True).start()

            @pl.when(jnp.logical_and(at >= 1, at <= turn))
            def _(way=way, block=turn - at):
                self.copy(way, piece, block).wait_recv()
                if forward:
                    slot = self.slots.at[way, piece, block]
                    own = self.own(way, piece, block)
                    slot[...] = (slot[...].astype(F32) + own[...].astype(F32)).astype(BF)
                    self.copy(way, piece, block).start()

    def result(self, piece, out):
        m, nm = self.geo.m, self.geo.nm
        own = self.part[piece, pl.ds(pl.multiple_of(m * self.span, self.span), self.span), :]
        out[piece] = own.astype(F32)

        @pl.when(m >= 1)
        def _():
            out[piece] = out[piece] + self.slots[0, piece, nm - 1 - m].astype(F32)

        @pl.when(m <= nm - 2)
        def _():
            out[piece] = out[piece] + self.slots[1, piece, m].astype(F32)

    def finish(self, piece):
        nm = self.geo.nm
        for way in range(2):
            at = self.place(way)
            for block in range(nm - 1):
                first = 0 if block == nm - 2 else 1

                @pl.when(jnp.logical_and(at >= first, at <= nm - 2 - block))
                def _(way=way, block=block):
                    self.copy(way, piece, block).wait_send()


def comm_params(collective, limit=60):
    return pltpu.CompilerParams(
        collective_id=collective, has_side_effects=True, vmem_limit_bytes=limit * 2**20
    )


def load(pairs):
    for src, dst, sem in pairs:
        pltpu.make_async_copy(src, dst, sem).start()


def ready(pairs):
    for src, dst, sem in pairs:
        pltpu.make_async_copy(src, dst, sem).wait()


GROUP = 4


def conv_row(conv, group, tap, column):
    return conv[group, pl.ds(tap, 1), pl.ds(pl.multiple_of(column, LANES), LANES)]


def before_silu(extended, conv, piece, group, head, width, rank):
    span = extended.shape[1] - LEAD
    cols = pl.ds(pl.multiple_of(group * width + head * LANES, LANES), LANES)
    total = None
    for tap in range(4):
        term = conv_row(conv, group, tap, rank * width + head * LANES) * extended[
            piece, pl.ds(LEAD - tap, span), cols
        ]
        total = term if total is None else total + term
    return total


def strengths_of(geo, logits, lengths, bias, local_heads, piece):
    span = logits.shape[1]
    lane = iota((span, LANES), 1)
    offset = jnp.zeros((span, LANES), F32)
    for head in range(local_heads):
        offset = jnp.where(lane == head, bias[geo.m * local_heads + head], offset)
    position = geo.s * span + iota((span, LANES), 0)
    live = jnp.where(position < lengths[piece], 1.0, 0.0)
    return sigmoid(logits[piece] + offset), live


def column_of(values, head):
    return jnp.sum(jnp.where(iota(values.shape, 1) == head, values, 0.0), -1, keepdims=True)


def fill_extended(extended, projected, edge, piece):
    extended[piece, LEAD:, :] = projected[piece].astype(F32)
    extended[piece, :LEAD, :] = edge[piece, EDGE - LEAD :, :].astype(F32)


class Chains:
    @staticmethod
    def scratch(ns, chains):
        return [
            pltpu.VMEM((ns, LANES, LANES), F32),
            DMA((chains,)), DMA((ns,)), DMA((ns,)), DMA((chains,)),
        ]

    def __init__(self, geo, chains, pair, links, entries, scratch):
        self.geo, self.chains = geo, chains
        self.pair, self.links, self.entries = pair, links, entries
        self.states, self.pair_send, self.pair_recv, self.back_send, self.back_recv = scratch
        self.stride = geo.ns // chains
        self.mine = geo.s // self.stride
        self.holds = geo.s == self.mine * self.stride

    def link_copy(self, chain):
        s, m = self.geo.s, self.geo.m
        return remote(
            self.pair.at[chain], self.links.at[s], self.pair_send.at[chain], self.pair_recv.at[s],
            (chain * self.stride, m),
        )

    def give(self, chain, link):
        owner = chain * self.stride

        @pl.when(owner == self.geo.s)
        def _():
            self.links[self.geo.s] = link

        @pl.when(owner != self.geo.s)
        def _():
            self.link_copy(chain).start()

    def state_copy(self, other):
        return remote(
            self.states.at[other], self.entries.at[self.mine], self.back_send.at[other],
            self.back_recv.at[self.mine], (other, self.geo.m),
        )

    def run(self, first, count, advance, start, reverse, last):
        ns, s, m = self.geo.ns, self.geo.s, self.geo.m

        @pl.when(jnp.logical_and(self.holds, jnp.logical_and(self.mine >= first, self.mine < first + count)))
        def _():
            def step(lap, carry):
                at = ns - 1 - lap if reverse else lap
                state = carry[0]
                self.states[at] = state

                @pl.when(at == s)
                def _():
                    self.entries[self.mine] = state

                @pl.when(at != s)
                def _():
                    self.state_copy(at).start()
                    remote(
                        self.pair.at[0], self.links.at[at], self.pair_send.at[0],
                        self.pair_recv.at[at], (s, m),
                    ).wait_recv()

                return advance(carry, at)

            last(lax.fori_loop(0, ns, step, start))

    def receive(self, chain):
        @pl.when(chain * self.stride != self.geo.s)
        def _():
            remote(
                self.states.at[0], self.entries.at[chain], self.back_send.at[0],
                self.back_recv.at[chain], (self.geo.s, self.geo.m),
            ).wait_recv()

    def finish(self):
        def sent(chain, carry):
            @pl.when(chain * self.stride != self.geo.s)
            def _():
                self.link_copy(chain).wait_send()

            return carry

        lax.fori_loop(0, self.chains, sent, 0)

        @pl.when(self.holds)
        def _():
            def done(other, carry):
                @pl.when(other != self.geo.s)
                def _():
                    self.state_copy(other).wait_send()

                return carry

            lax.fori_loop(0, self.geo.ns, done, 0)


def mixer_kernel(
    sizes, tokens, cotangent, query_w, key_w, value_w, beta_w, out_in, gate_hbm, up_hbm, down_in,
    conv, lengths, bias, mixer_gain, head_gain, feed_gain,
    rows_o, proj_w_o, out_w_o, gate_w_o, up_w_o, down_w_o, grad_rows_o, feed_rows_o,
    hidden_in, head_rows, projected, logits, edge, links, norm_o, entry_o,
    solve_h, wkeys_h, fresh_h, error_h, outputs_h, queries_h, keys_h,
    solve_o, wkeys_o, fresh_o, error_o, outputs_o, queries_o, keys_o,
    proj_shard, out_shard, gate_shard, up_shard, down_shard,
    rows, weight, out_w, grad_rows, feed_rows, part, extended, betas, wvalues, pair,
    keep, edge_send, edge_recv, *rest,
):
    geo = Geo(sizes)
    ns, nm, s, m = geo.ns, geo.nm, geo.s, geo.m
    mates = line_mates(geo) + all_mates(geo)
    greet(mates)
    shards = [(gate_hbm, gate_shard, keep.at[0]), (up_hbm, up_shard, keep.at[1])]
    load(shards)
    width = query_w.shape[1]
    heads = width // LANES
    chains = NSEQ * heads
    span = projected.shape[1]
    proj_shard[:, 0:width] = query_w[...]
    proj_shard[:, width : 2 * width] = key_w[...]
    proj_shard[:, 2 * width : 3 * width] = value_w[...]
    proj_shard[:, 3 * width :] = jnp.zeros((proj_shard.shape[0], LANES), BF)
    proj_shard[:, 3 * width : 3 * width + heads] = beta_w[...]
    out_shard[...] = out_in[...].T
    await_all(mates)

    weights = CubeGather(geo, proj_shard, weight, rest[0:3])
    outs = CubeGather(geo, out_shard, out_w, rest[3:6])
    gates = CubeGather(geo, gate_shard, gate_w_o, rest[6:9])
    ups = CubeGather(geo, up_shard, up_w_o, rest[9:12])
    downs = CubeGather(geo, down_shard, down_w_o, rest[12:15])
    spread = LineGather(geo, rows, rest[15:17])
    spread_grad = LineGather(geo, grad_rows, rest[17:19])
    spread_feed = LineGather(geo, feed_rows, rest[19:21])
    collect = LineScatter(geo, part, rest[21:24])
    chain = Chains(geo, chains, pair, links, entry_o, rest[24:29])

    weights.begin()
    own_rows = tokens.shape[1]
    mine = pl.ds(pl.multiple_of(m * own_rows, own_rows), own_rows)
    for piece in range(NSEQ):
        values = tokens[piece].astype(F32)
        rows[piece, mine, :] = (values * row_scale(values) * mixer_gain[...]).astype(BF)
        grad_rows[piece, mine, :] = cotangent[piece]
        if piece == 0:
            spread.begin(0)
    down_shard[...] = down_in[...].T
    spread.advance(0, 0)
    spread.begin(1)
    weights.advance(2)
    outs.begin()
    for hop in range(1, nm - 1):
        spread.advance(0, hop)
        weights.advance(2)
        spread.advance(1, hop - 1)
    outs.advance(2)
    weights.settle()
    ready(shards)
    kept = [(weight, proj_w_o, keep.at[2])]
    load(kept)
    strict = lower_mask(span, True)
    whole = lower_mask(span, False)
    norm_o[...] = jnp.zeros(norm_o.shape, F32)

    def edge_copy(piece):
        return remote(
            projected.at[piece, pl.ds(span - EDGE, EDGE)], edge.at[piece],
            edge_send.at[piece], edge_recv.at[piece], (s + 1, m),
        )

    def run_chains(piece):
        def advance(carry, at):
            state, total = carry
            link = links[at]
            high, low = halves(state)
            move = link[:, :LANES]
            state = state - (dot(move, high) + dot(move, low)) + link[:, LANES:].astype(F32)
            return state, total + jnp.sqrt(jnp.sum(state * state, (0, 1), keepdims=True))

        def last(carry):
            norm_o[...] = norm_o[...] + carry[1]

        start = (jnp.zeros((LANES, LANES), F32), jnp.zeros((1, 1), F32))
        chain.run(piece * heads, heads, advance, start, False, last)

    groups = heads // GROUP

    def solve(piece, carry):
        @pl.when(piece == 1)
        def _():
            for hop in range(nm - 2, nm - 1):
                spread.advance(1, hop)

        result = dot(rows[piece], weight[...])
        projected[piece] = result[:, : 3 * width].astype(BF)
        logits[piece] = result[:, 3 * width :]

        @pl.when(s < ns - 1)
        def _():
            edge_copy(piece).start()

        strength, live = strengths_of(geo, logits, lengths, bias, heads, piece)
        betas[piece] = strength * live

        @pl.when(piece == 0)
        def _():
            gates.begin((0,))
            for at in range(NSEQ):
                spread_grad.begin(at)

        @pl.when(piece == 1)
        def _():
            gates.begin(range(1, len(gates.orders[0])))

        @pl.when(s > 0)
        def _():
            edge_copy(piece).wait_recv()

        @pl.when(s == 0)
        def _():
            edge[piece] = jnp.zeros(edge.shape[1:], BF)

        fill_extended(extended, projected, edge, piece)
        for first in range(0, heads, GROUP):
            which = [first + k for k in range(GROUP)]
            mixed = [
                [before_silu(extended, conv, piece, g, head, width, m) for g in range(3)]
                for head in which
            ]
            mixed = [[z * sigmoid(z) for z in three] for three in mixed]
            queries = [three[0] for three in mixed]
            keys = [
                key * lax.rsqrt(jnp.sum(key * key, -1, keepdims=True) + KEY_EPSILON)
                for _, key, _ in mixed
            ]
            values = [three[2] for three in mixed]
            strengths = [column_of(betas[piece], head) for head in which]
            key_pairs = [halves(key) for key in keys]
            grams = [jnp.where(strict, fine(key, key, NT), 0.0) for key in key_pairs]
            inverses = unit_lower_inverses([gram * beta for gram, beta in zip(grams, strengths)])
            both = [
                halves(jnp.concatenate((key * beta, value * beta), 1))
                for key, value, beta in zip(keys, values, strengths)
            ]
            both = [fine(halves(inverse), right) for inverse, right in zip(inverses, both)]
            found = [fine(key, halves(two), TN).astype(BF) for key, two in zip(key_pairs, both)]
            done = list(zip(queries, keys, values, inverses, both, found))
            for k, (query, key, value, inverse, both, link) in enumerate(done):
                at = piece * heads + first + k
                pair[at] = link
                solve_o[at] = inverse
                wkeys_o[at] = both[:, :LANES]
                wvalues[at] = both[:, LANES:]
                queries_o[at] = query
                keys_o[at] = key
                error_o[at] = value
            for k, found in enumerate(done):
                chain.give(piece * heads + first + k, found[-1])
        return carry

    lax.fori_loop(0, NSEQ, solve, 0)
    saved = [
        (solve_o, solve_h, keep.at[7]), (wkeys_o, wkeys_h, keep.at[8]),
        (queries_o, queries_h, keep.at[9]), (keys_o, keys_h, keep.at[10]),
    ]
    load(saved)
    for piece in range(NSEQ):
        spread_grad.advance(piece, 0)
    outs.settle()
    for piece in range(NSEQ):
        run_chains(piece)

    def gates_on():
        gates.advance(4)
        ups.begin()
        downs.begin()

    def apply(piece, then=None):
        def step(lap, carry):
            first = piece * heads + lap * GROUP
            for k in range(GROUP):
                chain.receive(first + k)
            if then is not None:
                then()
            which = [first + k for k in range(GROUP)]
            states = [halves(entry_o[at]) for at in which]
            key_pairs = [halves(keys_o[at]) for at in which]
            query_pairs = [halves(queries_o[at]) for at in which]
            fresh = [
                wvalues[at] - fine(halves(wkeys_o[at]), state) for at, state in zip(which, states)
            ]
            fresh_pairs = [halves(one) for one in fresh]
            grams = [jnp.where(strict, fine(key, key, NT), 0.0) for key in key_pairs]
            scores = [
                jnp.where(whole, fine(query, key, NT), 0.0)
                for query, key in zip(query_pairs, key_pairs)
            ]
            errors = [
                error_o[at] - fine(key, state) - fine(halves(gram), new)
                for at, key, state, gram, new in zip(which, key_pairs, states, grams, fresh_pairs)
            ]
            outputs = [
                fine(query, state) + fine(halves(score), new)
                for query, state, score, new in zip(query_pairs, states, scores, fresh_pairs)
            ]
            done = list(zip(fresh, errors, outputs))
            for k, (fresh, error, output) in enumerate(done):
                at = first + k
                fresh_o[at] = fresh
                error_o[at] = error
                outputs_o[at] = output
                cols = pl.ds(pl.multiple_of((lap * GROUP + k) * LANES, LANES), LANES)
                head_rows[piece, :, cols] = (output * row_scale(output) * head_gain[...]).astype(BF)
            return carry

        lax.fori_loop(0, groups, step, 0)
        part[piece] = dot(head_rows[piece], out_w[...], NT).astype(BF)

    def close(piece):
        collect.result(piece, hidden_in)
        values = hidden_in[piece] + tokens[piece].astype(F32)
        hidden_in[piece] = values
        feed_rows[piece, mine, :] = (values * row_scale(values) * feed_gain[...]).astype(BF)
        spread_feed.begin(piece)

    apply(0)
    collect.begin(0)
    for piece in range(NSEQ):
        spread_grad.advance(piece, 1)
    apply(1, gates_on)
    kept.append((out_w, out_w_o, keep.at[4]))
    later = [
        (fresh_o, fresh_h, keep.at[11]), (error_o, error_h, keep.at[12]),
        (outputs_o, outputs_h, keep.at[13]),
    ]
    load(kept[-1:] + later)
    collect.advance(0, 1)
    for piece in range(NSEQ):
        for hop in range(2, nm - 2):
            spread_grad.advance(piece, hop)
    collect.advance(0, 2)
    collect.begin(1)
    for turn in range(3, nm):
        collect.advance(0, turn)
    close(0)
    collect.advance(1, 1)
    gates.advance(2)
    spread_feed.advance(0, 0)
    collect.advance(1, 2)
    gates.advance()
    spread_feed.advance(0, 1)
    for turn in range(3, nm):
        collect.advance(1, turn)
    close(1)
    ups.advance(4)
    downs.advance(4)
    for hop in range(2, nm - 1):
        spread_feed.advance(0, hop)
    for piece in range(NSEQ):
        spread_grad.advance(piece, nm - 2)
    spread_feed.advance(1, 0)
    ups.advance(2)
    for hop in range(1, nm - 1):
        spread_feed.advance(1, hop)
    downs.advance(2)
    ups.advance()
    downs.advance()
    for piece in range(NSEQ):
        spread.finish(piece)
        collect.finish(piece)
        spread_grad.finish(piece)
        spread_feed.finish(piece)
    late = [
        (feed_rows, feed_rows_o, keep.at[5]), (grad_rows, grad_rows_o, keep.at[6]), (rows, rows_o, keep.at[3])
    ]
    load(late)
    for gather in (gates, ups, downs):
        gather.settle()
    for gather in (weights, outs, gates, ups, downs):
        gather.finish()
    for piece in range(NSEQ):
        @pl.when(s < ns - 1)
        def _(piece=piece):
            edge_copy(piece).wait_send()

    chain.finish()
    ready(kept + saved + later + late)


def mixer(
    sizes, tokens, cotangent, query_w, key_w, value_w, beta_w, out_in, gate_in, up_in, down_in,
    conv, lengths, bias, mixer_gain, head_gain, feed_gain,
):
    ns, nm = sizes
    width = query_w.shape[1]
    shard = query_w.shape[0]
    depth = ns * shard
    cols = gate_in.shape[1]
    own = tokens.shape
    span = own[1] * nm
    heads = width // LANES
    chains = NSEQ * heads
    rows = (NSEQ, span, depth)
    joined = 3 * width + LANES
    shape = jax.ShapeDtypeStruct
    per_chain = (chains, span, LANES)
    return pl.pallas_call(
        functools.partial(mixer_kernel, sizes),
        out_shape=(
            shape(rows, BF), shape((depth, joined), BF), shape((depth, width), BF),
            shape((depth, cols), BF), shape((depth, cols), BF), shape((depth, cols), BF),
            shape(rows, BF), shape(rows, BF),
            shape(own, F32), shape((NSEQ, span, width), BF), shape((NSEQ, span, 3 * width), BF),
            shape((NSEQ, span, LANES), F32), shape((NSEQ, EDGE, 3 * width), BF),
            shape((ns, LANES, 2 * LANES), BF), shape((8, LANES), F32),
            shape((chains, LANES, LANES), F32), shape((chains, span, span), F32),
        )
        + (shape(per_chain, F32),) * 6,
        in_specs=[VMEM] * 7 + [ANY, ANY, VMEM, VMEM, SMEM, SMEM, VMEM, VMEM, VMEM],
        out_specs=(ANY,) * 8 + (VMEM,) * 8 + (ANY,) * 7,
        scratch_shapes=[pltpu.VMEM((chains, span, span), F32)]
        + [pltpu.VMEM(per_chain, F32)] * 6
        + [
            pltpu.VMEM((shard, joined), BF), pltpu.VMEM((shard, width), BF),
            pltpu.VMEM((shard, cols), BF), pltpu.VMEM((shard, cols), BF), pltpu.VMEM((shard, cols), BF),
            pltpu.VMEM(rows, BF), pltpu.VMEM((depth, joined), BF), pltpu.VMEM((depth, width), BF),
            pltpu.VMEM(rows, BF), pltpu.VMEM(rows, BF), pltpu.VMEM(rows, BF),
            pltpu.VMEM((NSEQ, LEAD + span, 3 * width), F32),
            pltpu.VMEM((NSEQ, span, LANES), F32),
            pltpu.VMEM(per_chain, F32),
            pltpu.VMEM((chains, LANES, 2 * LANES), BF),
            DMA((14,)), DMA((NSEQ,)), DMA((NSEQ,)),
        ]
        + CubeGather.sems(ns) * 5
        + LineGather.sems(nm) * 3
        + LineScatter.scratch(nm, own[1], depth)
        + Chains.scratch(ns, chains),
        compiler_params=comm_params(0),
        name="mixer",
    )(
        tokens, cotangent, query_w, key_w, value_w, beta_w, out_in, gate_in, up_in, down_in,
        conv, lengths, bias, mixer_gain, head_gain, feed_gain,
    )


def feed_kernel(
    sizes, feed_rows, grad_rows, gate_hbm, up_hbm, down_hbm, hidden_in, gain, cotangent,
    grad_in, mix_rows_o, grad_gate_o, grad_up_o, grad_down_o, down_part_o, gain_o,
    gate_w, up_w, down_w, hidden, grad_gate, grad_up, part, mix_rows, keep, *rest,
):
    geo = Geo(sizes)
    nm = geo.nm
    weights = [
        (gate_hbm, gate_w, keep.at[0]), (up_hbm, up_w, keep.at[1]), (down_hbm, down_w, keep.at[2])
    ]
    load(weights)
    meet(line_mates(geo) + cube_mates(geo))
    collect = LineScatter(geo, part, rest[0:3])
    spread = LineGather(geo, mix_rows, rest[3:5])
    first = CubeScatter(geo, gate_w, rest[5:8])
    second = CubeScatter(geo, up_w, rest[8:11])
    for piece in range(NSEQ):
        if piece == 0:
            ready(weights[:1])
        gate = dot(feed_rows[piece], gate_w[...])
        if piece == 0:
            ready(weights[1:2])
        up = dot(feed_rows[piece], up_w[...])
        sig = sigmoid(gate)
        active = gate * sig
        hidden[piece] = (active * up).astype(BF)
        if piece == 0:
            ready(weights[2:3])
        grad_hidden = dot(grad_rows[piece], down_w[...])
        grad_gate[piece] = (grad_hidden * up * sig * (1.0 + gate * (1.0 - sig))).astype(BF)
        grad_up[piece] = (grad_hidden * active).astype(BF)
        part[piece] = (
            dot(grad_gate[piece], gate_w[...], NT) + dot(grad_up[piece], up_w[...], NT)
        ).astype(BF)
        if piece == 0:
            collect.begin(0)
    depth, cols = gate_w.shape
    tile = 512
    span = hidden_in.shape[1]
    mine = pl.ds(pl.multiple_of(geo.m * span, span), span)

    def weight_grad(rows, grads, out):
        def step(at, carry):
            window = pl.ds(pl.multiple_of(at * tile, tile), tile)
            total = dot(rows[0, :, window], grads[0], TN) + dot(rows[1, :, window], grads[1], TN)
            out[window, :] = total.astype(BF)
            return carry

        lax.fori_loop(0, depth // tile, step, 0)

    def close(piece):
        collect.result(piece, grad_in)
        grad_feed = grad_in[piece]
        rows = hidden_in[piece]
        scale = row_scale(rows)
        unit = rows * scale
        part_gain = jnp.sum(grad_feed * unit, 0, keepdims=True)
        if piece == 0:
            gain_o[...] = part_gain
        else:
            gain_o[...] = gain_o[...] + part_gain
        back = cotangent[piece].astype(F32) + norm_backward(grad_feed * gain[...], unit, scale)
        grad_in[piece] = back
        mix_rows[piece, mine, :] = back.astype(BF)
        spread.begin(piece)

    collect.advance(0, 1)
    weight_grad(feed_rows, grad_gate, gate_w)
    first.begin()
    collect.advance(0, 2)
    collect.begin(1)
    weight_grad(feed_rows, grad_up, up_w)
    first.advance(4)
    for turn in range(3, nm):
        collect.advance(0, turn)
    close(0)
    first.advance(4)
    collect.advance(1, 1)
    second.begin()
    spread.advance(0, 0)
    collect.advance(1, 2)
    second.advance(8)
    spread.advance(0, 1)
    first.advance(2)
    for turn in range(3, nm):
        collect.advance(1, turn)
    close(1)
    first.advance(2)
    for piece in range(NSEQ):
        collect.finish(piece)
        part[piece] = dot(hidden[piece], down_w[...], NT).astype(BF)
    later = [(part, down_part_o, keep.at[0])]
    load(later)
    for hop in range(2, nm - 1):
        spread.advance(0, hop)
    spread.advance(1, 0)
    weight_grad(grad_rows, hidden, down_w)
    later.append((down_w, grad_down_o, keep.at[1]))
    load(later[1:])
    second.advance(4)
    for hop in range(1, nm - 1):
        spread.advance(1, hop)
    for piece in range(NSEQ):
        spread.finish(piece)
    later.append((mix_rows, mix_rows_o, keep.at[2]))
    load(later[2:])
    first.finish(grad_gate_o)
    second.finish(grad_up_o)
    ready(later)


def feed(sizes, feed_rows, grad_rows, gate_w, up_w, down_w, hidden_in, gain, cotangent):
    ns, nm = sizes
    depth, cols = gate_w.shape
    span = hidden_in.shape[1]
    shard = depth // ns
    rows = (NSEQ, span * nm, depth)
    inner = (NSEQ, span * nm, cols)
    return pl.pallas_call(
        functools.partial(feed_kernel, sizes),
        out_shape=(
            jax.ShapeDtypeStruct((NSEQ, span, depth), F32),
            jax.ShapeDtypeStruct(rows, BF),
            jax.ShapeDtypeStruct((shard, cols), F32),
            jax.ShapeDtypeStruct((shard, cols), F32),
            jax.ShapeDtypeStruct((depth, cols), BF),
            jax.ShapeDtypeStruct(rows, BF),
            jax.ShapeDtypeStruct((1, depth), F32),
        ),
        in_specs=[VMEM, VMEM, ANY, ANY, ANY, VMEM, VMEM, VMEM],
        out_specs=(VMEM, ANY, VMEM, VMEM, ANY, ANY, VMEM),
        scratch_shapes=[
            pltpu.VMEM((depth, cols), BF), pltpu.VMEM((depth, cols), BF), pltpu.VMEM((depth, cols), BF),
            pltpu.VMEM(inner, BF), pltpu.VMEM(inner, BF), pltpu.VMEM(inner, BF),
            pltpu.VMEM(rows, BF), pltpu.VMEM(rows, BF), DMA((3,)),
        ]
        + LineScatter.scratch(nm, span, depth)
        + LineGather.sems(nm)
        + CubeScatter.scratch(ns, shard, cols) * 2,
        compiler_params=comm_params(1, 63),
        name="feed",
    )(feed_rows, grad_rows, gate_w, up_w, down_w, hidden_in, gain, cotangent)


def backward_kernel(
    sizes, mix_rows_h, out_weight_h, head_rows, projected, logits, conv, lengths, bias, gain,
    edge, links, solve_h, wkeys_h, fresh_h, error_h, outputs_h, queries_h, keys_h, entry,
    grad_down_hbm, down_part_hbm, hidden_in,
    grads_o, block_o, grad_out_o, grad_down_o, conv_o, gain_o, bias_o,
    mix_rows, out_weight, solve, fresh, error, queries, keys,
    extended, betas, grad_output, held, grad_mixed, grad_tail, grad_logit,
    pair, gathered, leaving, edge_out, edge_in, out_total, down_total, down_part, keep,
    edge_send, edge_recv, *rest,
):
    geo = Geo(sizes)
    ns, nm, s, m = geo.ns, geo.nm, geo.s, geo.m
    span, width = projected.shape[1], projected.shape[2] // 3
    heads = width // LANES
    chains = NSEQ * heads
    which = range(heads)
    mates = line_mates(geo) + all_mates(geo)
    greet(mates)
    loads = [
        (down_part_hbm, down_part, keep.at[0]), (grad_down_hbm, down_total, keep.at[1]),
        (mix_rows_h, mix_rows, keep.at[2]), (out_weight_h, out_weight, keep.at[3]),
        (outputs_h, grad_output, keep.at[4]), (queries_h, queries, keep.at[5]),
        (keys_h, keys, keep.at[6]), (wkeys_h, held, keep.at[7]),
        (fresh_h, fresh, keep.at[8]), (solve_h, solve, keep.at[9]), (error_h, error, keep.at[10]),
    ]
    load(loads)
    collect = LineScatter(geo, down_part, rest[0:3])
    first = CubeScatter(geo, down_total, rest[3:6])
    second = CubeScatter(geo, out_total, rest[6:9])
    chain = Chains(geo, chains, pair, gathered, leaving, rest[9:14])
    strict = lower_mask(span, True)
    whole = lower_mask(span, False)
    gain_o[...] = jnp.zeros(gain_o.shape, F32)
    conv_o[...] = jnp.zeros(conv_o.shape, F32)
    pad = grad_mixed.shape[1] - LEAD - span
    for piece in range(NSEQ):
        grad_mixed[piece, :LEAD, :] = jnp.zeros((LEAD, 3 * width), F32)
        grad_mixed[piece, LEAD + span :, :] = jnp.zeros((pad, 3 * width), F32)
        fill_extended(extended, projected, edge, piece)
        strength, live = strengths_of(geo, logits, lengths, bias, heads, piece)
        betas[piece] = strength * live
    await_all(mates)
    ready(loads[:2])
    for piece in range(NSEQ):
        collect.begin(piece)
    first.begin()
    ready(loads[2:8])

    def start(piece, carry):
        grad_head = dot(mix_rows[piece], out_weight[...])
        scaled = [grad_output[piece * heads + h] for h in which]
        scales = [row_scale(output) for output in scaled]
        units = [output * scale for output, scale in zip(scaled, scales)]
        grads = [grad_head[:, h * LANES : (h + 1) * LANES] for h in which]
        share = [jnp.sum(grad * unit, 0, keepdims=True) for grad, unit in zip(grads, units)]
        gain_o[...] = gain_o[...] + sum(share)
        grads = [
            norm_backward(grad * gain[...], unit, scale)
            for grad, unit, scale in zip(grads, units, scales)
        ]
        grad_pairs = [halves(grad) for grad in grads]
        query_pairs = [halves(queries[piece * heads + h]) for h in which]
        scores = [
            jnp.where(whole, fine(query, halves(keys[piece * heads + h]), NT), 0.0)
            for h, query in zip(which, query_pairs)
        ]
        spread = [fine(halves(score), grad, TN) for score, grad in zip(scores, grad_pairs)]
        found = [
            fine(query, grad, TN) - fine(halves(held[piece * heads + h]), halves(one), TN)
            for h, query, grad, one in zip(which, query_pairs, grad_pairs, spread)
        ]
        found = [link.astype(BF) for link in found]
        for h in which:
            at = piece * heads + h
            grad_output[at] = grads[h]
            held[at] = spread[h]
            pair[at] = found[h]
        for h in which:
            chain.give(piece * heads + h, found[h])
        return carry

    lax.fori_loop(0, NSEQ, start, 0)
    ready(loads[8:])

    def through_conv(piece, h, group, grad, key=None):
        z = before_silu(extended, conv, piece, group, h, width, m)
        sig = sigmoid(z)
        if key is not None:
            raw = z * sig
            scale = lax.rsqrt(jnp.sum(raw * raw, -1, keepdims=True) + KEY_EPSILON)
            grad = scale * (grad - key * jnp.sum(key * grad, -1, keepdims=True))
        grad = grad * sig * (1.0 + z * (1.0 - sig))
        cols = slice(group * width + h * LANES, group * width + (h + 1) * LANES)
        local = slice(h * LANES, (h + 1) * LANES)
        grad_mixed[piece, pl.ds(LEAD, span), cols] = grad
        back = None
        for tap in range(4):
            share = jnp.sum(grad * extended[piece, pl.ds(LEAD - tap, span), cols], 0, keepdims=True)
            row = slice(group * 4 + tap, group * 4 + tap + 1)
            conv_o[row, local] = conv_o[row, local] + share
            term = (
                conv_row(conv, group, tap, m * width + h * LANES)
                * grad_mixed[piece, pl.ds(tap, LEAD + span), cols]
            )
            back = term if back is None else back + term
        edge_out[piece, :, cols] = back[:LEAD]
        grads_o[piece, :, cols] = back[LEAD:].astype(BF)
        grad_tail[piece, :, cols] = back[LEAD + span - EDGE :]

    def before_exit(piece):
        base = piece * heads
        grad_pairs = [halves(grad_output[base + h]) for h in which]
        key_pairs = [halves(keys[base + h]) for h in which]
        scores = [
            halves(jnp.where(whole, fine(grad, halves(fresh[base + h]), NT), 0.0))
            for h, grad in zip(which, grad_pairs)
        ]
        grads = [
            fine(score, key) + fine(grad, halves(entry[base + h]), NT)
            for h, score, key, grad in zip(which, scores, key_pairs, grad_pairs)
        ]
        to_keys = [
            fine(score, halves(queries[base + h]), TN) for h, score in zip(which, scores)
        ]
        for h in which:
            grad_output[base + h] = to_keys[h]
        for h in which:
            through_conv(piece, h, 0, grads[h])

    def after_exit(piece):
        base = piece * heads
        for h in which:
            chain.receive(base + h)
        key_pairs = [halves(keys[base + h]) for h in which]
        exits = [halves(leaving[base + h]) for h in which]
        fresh_pairs = [halves(fresh[base + h]) for h in which]
        strengths = [column_of(betas[piece], h) for h in which]
        weak = [halves(held[base + h] + fine(key, out)) for h, key, out in zip(which, key_pairs, exits)]
        weak = [fine(halves(solve[base + h]), one, TN) for h, one in zip(which, weak)]
        grad_beta = [jnp.sum(one * error[base + h], -1, keepdims=True) for h, one in zip(which, weak)]
        values = [one * beta for one, beta in zip(weak, strengths)]
        value_pairs = [halves(value) for value in values]
        scores = [
            halves(jnp.where(strict, -fine(value, new, NT), 0.0))
            for value, new in zip(value_pairs, fresh_pairs)
        ]
        grads = [
            grad_output[base + h]
            - fine(value, halves(entry[base + h]), NT)
            + fine(score, key)
            + fine(score, key, TN)
            + fine(new, out, NT)
            for h, value, score, key, new, out in zip(
                which, value_pairs, scores, key_pairs, fresh_pairs, exits
            )
        ]
        lane = iota((span, LANES), 1)
        grad_logit[piece] = sum(jnp.where(lane == h, grad_beta[h], 0.0) for h in which)
        for h in which:
            through_conv(piece, h, 1, grads[h], keys[base + h])
            through_conv(piece, h, 2, values[h])

    def run_chains(piece):
        def advance(carry, at):
            (state,) = carry
            high, low = halves(state)
            move = links[at][:, :LANES]
            state = state - (dot(move, high, TN) + dot(move, low, TN)) + gathered[at].astype(F32)
            return (state,)

        chain.run(
            piece * heads, heads, advance, (jnp.zeros((LANES, LANES), F32),), True, lambda carry: None
        )

    def edge_copy(piece):
        return remote(
            edge_out.at[piece], edge_in.at[piece], edge_send.at[piece], edge_recv.at[piece],
            (s - 1, m),
        )

    depth = out_weight.shape[0]
    tile = 512

    def weight_grad(at, carry):
        window = pl.ds(pl.multiple_of(at * tile, tile), tile)
        total = dot(mix_rows[0, :, window], head_rows[0], TN) + dot(
            mix_rows[1, :, window], head_rows[1], TN
        )
        out_total[window, :] = total.astype(BF)
        return carry

    def leave(piece, carry):
        @pl.when(piece == 0)
        def _():
            first.advance(8)

        before_exit(piece)

        @pl.when(piece == 0)
        def _():
            for at in range(NSEQ):
                run_chains(at)
            for at in range(NSEQ):
                collect.advance(at, 1)
            lax.fori_loop(0, depth // tile, weight_grad, 0)
            second.begin()

        return carry

    lax.fori_loop(0, NSEQ, leave, 0)

    def enter(piece, carry):
        after_exit(piece)

        @pl.when(s > 0)
        def _():
            edge_copy(piece).start()

        @pl.when(piece == 0)
        def _():
            for at in range(NSEQ):
                collect.advance(at, 2)
            second.advance(8)
            first.advance(4)

        return carry

    lax.fori_loop(0, NSEQ, enter, 0)
    bias_sum = jnp.zeros((1, LANES), F32)
    for piece in range(NSEQ):
        sig, live = strengths_of(geo, logits, lengths, bias, heads, piece)
        grad = grad_logit[piece] * live * sig * (1.0 - sig)
        bias_sum = bias_sum + jnp.sum(grad, 0, keepdims=True)
        grads_o[piece, :, pl.ds(3 * width, LANES)] = grad.astype(BF)
    lane = iota((1, LANES), 1)
    spread_bias = jnp.zeros((1, LANES), F32)
    for h in which:
        spread_bias = spread_bias + jnp.where(lane == m * heads + h, column_of(bias_sum, h), 0.0)
    bias_o[...] = spread_bias
    second.advance(4)
    for turn in range(3, nm):
        for piece in range(NSEQ):
            collect.advance(piece, turn)
    for piece in range(NSEQ):
        collect.result(piece, block_o)
        block_o[piece] = block_o[piece] + hidden_in[piece]
        collect.finish(piece)

    for piece in range(NSEQ):
        @pl.when(s < ns - 1)
        def _(piece=piece):
            edge_copy(piece).wait_recv()
            tail = pl.ds(EDGE - LEAD, LEAD)
            grad_tail[piece, tail, :] = grad_tail[piece, tail, :] + edge_in[piece]
            grads_o[piece, pl.ds(span - EDGE, EDGE), pl.ds(0, 3 * width)] = grad_tail[piece].astype(BF)

        @pl.when(s > 0)
        def _(piece=piece):
            edge_copy(piece).wait_send()

    first.finish(grad_down_o)
    second.finish(grad_out_o)
    chain.finish()


def backward(
    sizes, mix_rows, out_weight, head_rows, projected, logits, conv, lengths, bias, gain, saved,
    grad_down, down_part, hidden_in,
):
    ns, nm = sizes
    span, width = projected.shape[1], projected.shape[2] // 3
    heads = width // LANES
    chains = NSEQ * heads
    depth, cols = grad_down.shape
    shard = depth // ns
    local = hidden_in.shape
    rows = (NSEQ, span, depth)
    per_chain = (chains, span, LANES)
    return pl.pallas_call(
        functools.partial(backward_kernel, sizes),
        out_shape=(
            jax.ShapeDtypeStruct((NSEQ, span, 3 * width + LANES), BF),
            jax.ShapeDtypeStruct(local, F32),
            jax.ShapeDtypeStruct((shard, width), F32),
            jax.ShapeDtypeStruct((shard, cols), F32),
            jax.ShapeDtypeStruct((12, width), F32),
            jax.ShapeDtypeStruct((1, LANES), F32),
            jax.ShapeDtypeStruct((1, LANES), F32),
        ),
        in_specs=[ANY, ANY] + [VMEM] * 4 + [SMEM, SMEM] + [VMEM] * 3 + [ANY] * 7 + [VMEM, ANY, ANY, VMEM],
        out_specs=(VMEM,) * 7,
        scratch_shapes=[
            pltpu.VMEM(rows, BF), pltpu.VMEM((depth, width), BF),
            pltpu.VMEM((chains, span, span), F32),
        ]
        + [pltpu.VMEM(per_chain, F32)] * 4
        + [
            pltpu.VMEM((NSEQ, LEAD + span, 3 * width), F32),
            pltpu.VMEM((NSEQ, span, LANES), F32),
            pltpu.VMEM(per_chain, F32),
            pltpu.VMEM(per_chain, F32),
            pltpu.VMEM((NSEQ, LEAD + span + LEAD, 3 * width), F32),
            pltpu.VMEM((NSEQ, EDGE, 3 * width), F32),
            pltpu.VMEM((NSEQ, span, LANES), F32),
            pltpu.VMEM((chains, LANES, LANES), BF),
            pltpu.VMEM((ns, LANES, LANES), BF),
            pltpu.VMEM((chains, LANES, LANES), F32),
            pltpu.VMEM((NSEQ, LEAD, 3 * width), F32),
            pltpu.VMEM((NSEQ, LEAD, 3 * width), F32),
            pltpu.VMEM((depth, width), BF),
            pltpu.VMEM((depth, cols), BF),
            pltpu.VMEM(rows, BF),
            DMA((11,)), DMA((NSEQ,)), DMA((NSEQ,)),
        ]
        + LineScatter.scratch(nm, local[1], depth)
        + CubeScatter.scratch(ns, shard, cols)
        + CubeScatter.scratch(ns, shard, width)
        + Chains.scratch(ns, chains),
        compiler_params=comm_params(2, 63),
        name="recurrence_back",
    )(
        mix_rows, out_weight, head_rows, projected, logits, conv, lengths, bias, gain, *saved,
        grad_down, down_part, hidden_in,
    )


def last_kernel(
    sizes, rows, grads, proj_w, tokens, gain, grad_in, conv_part, head_gain, bias, norms, feed_gain,
    grad_tokens, grad_weight_o, conv_o, head_gain_o, bias_o, norm_o, feed_gain_o, gain_o,
    part, total, vector, over_seq, over_mp,
    seq_send, seq_recv, mp_send, mp_recv, *rest,
):
    geo = Geo(sizes)
    ns, nm, s, m = geo.ns, geo.nm, geo.s, geo.m
    mates = [(s, (m + k) % nm) for k in range(1, nm)] + all_mates(geo)
    greet(mates)
    depth = proj_w.shape[0]
    width = vector.shape[1]
    wide = depth // width
    row = conv_part.shape[0]
    vector[...] = jnp.zeros(vector.shape, F32)
    vector[0:row, :] = conv_part[...]
    vector[row : row + 1, 0:LANES] = head_gain[...]
    vector[row : row + 1, LANES : 2 * LANES] = bias[...]
    vector[row : row + 1, 2 * LANES : 3 * LANES] = norms[0:1, :]
    for at in range(wide):
        vector[row + 1 + at : row + 2 + at, :] = feed_gain[:, at * width : (at + 1) * width]
    await_all(mates)
    collect = LineScatter(geo, part, rest[0:3])
    scatter = CubeScatter(geo, total, rest[3:6])
    shares = []

    def spread(piece):
        value = dot(grads[piece], proj_w[...], NT)
        part[piece] = value.astype(BF)
        collect.begin(piece)
        shares.append(jnp.sum(value * rows[piece].astype(F32), 0, keepdims=True))

    tile = 512

    def weight_grad(at, carry):
        window = pl.ds(pl.multiple_of(at * tile, tile), tile)
        value = dot(rows[0, :, window], grads[0], TN) + dot(rows[1, :, window], grads[1], TN)
        total[window, :] = value.astype(BF)
        return carry

    spread(0)
    lax.fori_loop(0, depth // tile, weight_grad, 0)
    scatter.begin()
    spread(1)
    share = (shares[0] + shares[1]) / gain[...]
    for at in range(wide):
        vector[row + 1 + wide + at : row + 2 + wide + at, :] = share[:, at * width : (at + 1) * width]

    def seq_copy(k):
        return remote(
            vector, over_seq.at[k], seq_send.at[k], seq_recv.at[k], ((s + 1 + k) % ns, m)
        )

    def mp_copy(k):
        return remote(
            over_mp.at[0], over_mp.at[1 + k], mp_send.at[k], mp_recv.at[k], (s, (m + 1 + k) % nm)
        )

    def seq_start(k, carry):
        seq_copy(k).start()
        return carry

    lax.fori_loop(0, ns - 1, seq_start, 0)
    collect.advance(0, 1)
    scatter.advance(8)

    def seq_add(k, value):
        seq_copy(k).wait_recv()
        return value + over_seq[k]

    over_mp[0] = lax.fori_loop(0, ns - 1, seq_add, vector[...])
    for k in range(nm - 1):
        mp_copy(k).start()
    collect.advance(1, 1)
    for turn in range(2, nm):
        for piece in range(NSEQ):
            collect.advance(piece, turn)
        if turn == 2:
            for k in range(nm - 1):
                mp_copy(k).wait_recv()
            scatter.advance(2)
    for piece in range(NSEQ):
        collect.result(piece, grad_tokens)
        values = tokens[piece].astype(F32)
        scale = row_scale(values)
        grad_tokens[piece] = grad_in[piece] + norm_backward(
            grad_tokens[piece] * gain[...], values * scale, scale
        )
        collect.finish(piece)
    for k in range(nm):
        origin = (m + nm - k) % nm
        cols = pl.ds(pl.multiple_of(origin * width, width), width)
        for group in range(3):
            for tap in range(4):
                at = group * 4 + tap
                conv_o[group, tap : tap + 1, cols] = over_mp[k, at : at + 1, :]
    summed = over_mp[0]
    for k in range(1, nm):
        summed = summed + over_mp[k]
    head_gain_o[...] = summed[row : row + 1, 0:LANES]
    bias_o[...] = summed[row : row + 1, LANES : 2 * LANES]
    norm_o[...] = summed[row : row + 1, 2 * LANES : 3 * LANES] / (NSEQ * HEADS * ns)
    for at in range(wide):
        cols = slice(at * width, (at + 1) * width)
        feed_gain_o[:, cols] = summed[row + 1 + at : row + 2 + at, :]
        gain_o[:, cols] = summed[row + 1 + wide + at : row + 2 + wide + at, :]
    scatter.finish(grad_weight_o)

    def seq_done(k, carry):
        seq_copy(k).wait_send()
        return carry

    lax.fori_loop(0, ns - 1, seq_done, 0)
    for k in range(nm - 1):
        mp_copy(k).wait_send()


def last(sizes, rows, grads, proj_w, tokens, gain, grad_in, small):
    ns, nm = sizes
    depth, cols = proj_w.shape
    span = tokens.shape[1]
    shard = depth // ns
    width = (cols - LANES) // 3
    vector = (-(-(13 + 2 * (depth // width)) // 8) * 8, width)
    shape = jax.ShapeDtypeStruct
    line = shape((1, LANES), F32)
    return pl.pallas_call(
        functools.partial(last_kernel, sizes),
        out_shape=(
            shape(grad_in.shape, F32), shape((shard, cols), F32), shape((3, 4, depth), F32),
            line, line, line, shape((1, depth), F32), shape((1, depth), F32),
        ),
        in_specs=[VMEM] * 11,
        out_specs=(VMEM,) * 8,
        scratch_shapes=[
            pltpu.VMEM(rows.shape, BF),
            pltpu.VMEM((depth, cols), BF),
            pltpu.VMEM(vector, F32),
            pltpu.VMEM((ns - 1,) + vector, F32),
            pltpu.VMEM((nm,) + vector, F32),
            DMA((ns - 1,)), DMA((ns - 1,)), DMA((nm - 1,)), DMA((nm - 1,)),
        ]
        + LineScatter.scratch(nm, span, depth)
        + CubeScatter.scratch(ns, shard, cols),
        compiler_params=comm_params(3),
        name="last",
    )(rows, grads, proj_w, tokens, gain, grad_in, *small)


def deliver_kernel(
    block, grad_tokens, grad_proj, grad_gate, grad_up, grad_down, grad_out, conv, *rest
):
    lines, rest = rest[:5], rest[5:]
    (
        block_o, grad_tokens_o, query_o, key_o, value_o, grad_gate_o, grad_up_o, beta_o, grad_down_o,
        grad_out_o, conv_o,
    ) = rest[:11]
    line_os, rest = rest[11:16], rest[16:]
    block_v, tokens_v, proj_v, gate_v, up_v, down_v, out_v, down_t, out_t, conv_v = rest[:10]
    line_vs, sems = rest[10:15], rest[15]
    width = query_o.shape[1]
    coming = [
        (src, held, sems.at[k])
        for k, (src, held) in enumerate(
            (
                (grad_down, down_v), (grad_out, out_v), (grad_gate, gate_v), (grad_up, up_v),
                (block, block_v), (grad_tokens, tokens_v), (grad_proj, proj_v), (conv, conv_v),
            )
            + tuple(zip(lines, line_vs))
        )
    ]
    load(coming)
    going = []

    def send(held, dst):
        going.append((held, dst, sems.at[len(coming) + len(going)]))
        load(going[-1:])

    ready(coming[0:2])
    down_t[...] = down_v[...].T
    send(down_t, grad_down_o)
    out_t[...] = out_v[...].T
    send(out_t, grad_out_o)
    ready(coming[2:6])
    send(gate_v, grad_gate_o)
    send(up_v, grad_up_o)
    send(block_v, block_o)
    send(tokens_v, grad_tokens_o)
    ready(coming[6:])
    for k, dst in enumerate((query_o, key_o, value_o)):
        send(proj_v.at[:, pl.ds(k * width, width)], dst)
    beta_o[...] = proj_v[:, 3 * width :].T[: beta_o.shape[0], :]
    conv_o[...] = conv_v[...]
    for line, dst in zip(line_vs, line_os):
        dst[...] = line[:, : dst.shape[1]]
    ready(going)


def deliver(block, grad_tokens, grad_proj, grad_gate, grad_up, grad_down, grad_out, conv, lines, counts):
    shard, cols = grad_gate.shape
    width = (grad_proj.shape[1] - LANES) // 3
    heads = width // LANES
    shape = jax.ShapeDtypeStruct
    square = shape((shard, width), F32)
    wide = shape((shard, cols), F32)
    there = pl.BlockSpec(memory_space=pltpu.HBM)
    held = [
        block.shape, grad_tokens.shape, grad_proj.shape, (shard, cols), (shard, cols), (shard, cols),
        (shard, width), (cols, shard), (width, shard), conv.shape,
    ] + [line.shape for line in lines]
    return pl.pallas_call(
        deliver_kernel,
        out_shape=(
            shape(block.shape, F32), shape(grad_tokens.shape, F32), square, square, square, wide, wide,
            shape((heads, shard), F32), shape((cols, shard), F32), shape((width, shard), F32),
            shape(conv.shape, F32),
        )
        + tuple(shape((1, count), F32) for count in counts),
        in_specs=[there] * 13,
        out_specs=(there,) * 7 + (VMEM, there, there) + (VMEM,) * 6,
        scratch_shapes=[pltpu.VMEM(dims, F32) for dims in held] + [DMA((24,))],
        compiler_params=pltpu.CompilerParams(vmem_limit_bytes=63 * 2**20),
        name="deliver",
    )(block, grad_tokens, grad_proj, grad_gate, grad_up, grad_down, grad_out, conv, *lines)


def on_device(
    sizes,
    tokens,
    lengths,
    mixer_gain,
    query_weight,
    key_weight,
    value_weight,
    beta_weight,
    beta_bias,
    conv_weight,
    head_gain,
    out_weight,
    feed_gain,
    gate_weight,
    up_weight,
    down_weight,
    cotangent,
):
    ns, nm = sizes
    depth = tokens.shape[2]
    width = query_weight.shape[1]
    heads = width // LANES
    mixer_gain_row = mixer_gain.reshape(1, depth)
    feed_gain_row = feed_gain.reshape(1, depth)
    head_gain_row = head_gain.reshape(1, LANES)
    (
        rows, proj_w, out_w, gate_w, up_w, down_w, grad_rows, feed_rows,
        hidden_in, head_rows, projected, logits, edge, links, norms, entry, *saved,
    ) = mixer(
        sizes, tokens, cotangent, query_weight, key_weight, value_weight, beta_weight, out_weight,
        gate_weight, up_weight, down_weight, conv_weight, lengths, beta_bias, mixer_gain_row,
        head_gain_row, feed_gain_row,
    )
    grad_in, mix_rows, grad_gate, grad_up, grad_down_part, down_part, feed_gain_part = feed(
        sizes, feed_rows, grad_rows, gate_w, up_w, down_w, hidden_in, feed_gain_row, cotangent
    )
    grads, block_output, grad_out, grad_down, conv_part, gain_part, bias_part = backward(
        sizes, mix_rows, out_w, head_rows, projected, logits, conv_weight, lengths, beta_bias,
        head_gain_row, (edge, links, *saved, entry), grad_down_part, down_part, hidden_in,
    )
    grad_tokens, grad_proj_w, conv_grad, gain_grad, bias_grad, norm, feed_gain_grad, mixer_grad = last(
        sizes, rows, grads, proj_w, tokens, mixer_gain_row, grad_in,
        (conv_part, gain_part, bias_part, norms, feed_gain_part),
    )
    (
        block_output, grad_tokens, grad_query, grad_key, grad_value, grad_gate, grad_up, grad_beta,
        grad_down, grad_out, conv_grad, mixer_grad, feed_gain_grad, gain_grad, bias_grad, norm,
    ) = deliver(
        block_output, grad_tokens, grad_proj_w, grad_gate, grad_up, grad_down, grad_out, conv_grad,
        (mixer_grad, feed_gain_grad, gain_grad, bias_grad, norm), (depth, depth, LANES, nm * heads, 1),
    )
    return (
        block_output,
        grad_tokens,
        mixer_grad.reshape(depth),
        grad_query,
        grad_key,
        grad_value,
        grad_beta.T,
        bias_grad.reshape(nm * heads),
        conv_grad,
        gain_grad.reshape(LANES),
        grad_out,
        feed_gain_grad.reshape(depth),
        grad_gate,
        grad_up,
        grad_down,
        norm[0, 0],
    )


def solution(mesh):
    sizes = (mesh.shape["seq"], mesh.shape["mp"])
    by_rows = P("seq", "mp")
    by_cols = P("mp", "seq")
    placed = P(None, ("seq", "mp"), None)
    return jax.shard_map(
        functools.partial(on_device, sizes),
        mesh=mesh,
        in_specs=(
            placed, P(), P(), by_rows, by_rows, by_rows, by_rows, P(), P(), P(), by_cols, P(),
            by_rows, by_rows, by_cols, placed,
        ),
        out_specs=(
            placed, placed, P(), by_rows, by_rows, by_rows, by_rows, P(), P(), P(), by_cols, P(),
            by_rows, by_rows, by_cols, P(),
        ),
        check_vma=False,
    )
```

time: 2040 us -> 369 us (0.18)
  waiting for transfers between devices: 1280 us -> 0 us
  matrix products: 493 us -> 0 us
  Pallas kernels: 0 us -> 361 us
  local copies, waits for them, and re-layouts: 119 us -> 1.43 us
  other arithmetic: 57.5 us -> 0 us
  blocking collectives: 54.1 us -> 0 us
    reduce_scatter x11 -> x0, waiting for transfers between devices: 713 us -> none  [the longest x4 221 us: collect_rows(): return lax.psum_scatter(values, 'mp', scatter_dimension=1, tiled=True)]
    dot_general x360 -> x0, matrix products: 493 us -> none  [the longest x304 342 us: matmul_high(): return jnp.matmul(left, right, precision=HIGHEST)]
    all_gather x15 -> x0, waiting for transfers between devices: 431 us -> none  [the longest x4 127 us: spread_rows(): return lax.all_gather(values, 'mp', axis=1, tiled=True)]
    pallas_call x0 -> x5, Pallas kernels: none -> 361 us  [the longest x1 147 us: mixer(): pl.pallas_call(functools.partial(mixer_kernel, sizes), out_shape=(shape(r...]
    psum x1 -> x0, waiting for transfers between devices: 128 us -> none  [on_device(): lax.psum((mixer_gain_part, feed_gain_part, grads[4], bias_full, conv_full...]
    psum x1 -> x0, blocking collectives: 43.6 us -> none  [on_device(): lax.psum((mixer_gain_part, feed_gain_part, grads[4], bias_full, conv_full...]
    another operation x33 -> x0, local copies, waits for them, and re-layouts: 35.4 us -> none
    reduce_sum x18 -> x0, other arithmetic: 26.5 us -> none  [the longest x3 5.02 us: finish_heads(): normed = outputs * row_scale(outputs) * gain_head]
  transfers between devices with their start and end apart: 30 -> 0, of which waited for: 24 -> 0; matrix products, arithmetic and copies ran while one was open for 17% -> 0% of each run, Pallas kernels for 0% -> 0%
where the time goes in v1:
time: 369 us; the launch traced here: 363 us
  Pallas kernels  361 us (98%)
    pallas_call x1, Pallas kernels, mixer(): pl.pallas_call(functools.partial(mixer_kernel, sizes), out_shape=(shape(r...  147 us
    pallas_call x1, Pallas kernels, feed(): pl.pallas_call(functools.partial(feed_kernel, sizes), out_shape=(jax.Shap...  91.1 us
    pallas_call x1, Pallas kernels, backward(): pl.pallas_call(functools.partial(backward_kernel, sizes), out_shape=(jax....  62.9 us
    pallas_call x1, Pallas kernels, last(): pl.pallas_call(functools.partial(last_kernel, sizes), out_shape=(shape(gr...  52.9 us

profile of v1, /device:TPU:0, one launch (start us, length us, event | category | flops | bytes accessed | tf_op | source)
XLA Modules:
  0.0 363.4 jit_solution(15742013142569603351)
XLA Ops:
  0.6 1.4 copy.32.beta_w
  2.1 147.0 %mixer.1 = (bf16[2,256,2048]{2,1,0:T(8,128)(2,1)}, bf16[2048,1664]{1,0:T(8,128)(2,1)}, bf16[2048,512]{1,0:T(8,128)(2,1)}, bf16[2048,1408]{1,0:T(8,128)(2,1)}, bf...) custom-call(bf16[2,64,2048]{2,1,0:T(8,128)(2,1)} %tokens.3, ...), custom_call_target="tpu_custom_call" | custom-call | tf_op jit(solution)/shard_map/mixer/pallas_call | solution.py:925
  149.0 91.1 %feed.1 = (f32[2,64,2048]{2,1,0:T(8,128)}, bf16[2,256,2048]{2,1,0:T(8,128)(2,1)}, f32[256,1408]{1,0:T(8,128)}, f32[256,1408]{1,0:T(8,128)}, bf16[2048,1408]{1,0:...) custom-call(bf16[2,256,2048]{2,1,0:T(8,128)(2,1)} %get-tuple-element.77.feed_rows, ...), custom_call_target="tpu_custom_call" | custom-call | tf_op jit(solution)/shard_map/feed/pallas_call | solution.py:1082
  240.2 62.9 %recurrence_back.1 = (bf16[2,256,1664]{2,1,0:T(8,128)(2,1)}, f32[2,64,2048]{2,1,0:T(8,128)}, f32[256,512]{1,0:T(8,128)}, f32[256,1408]{1,0:T(8,128)}, f32[12,512...) custom-call(bf16[2,256,2048]{2,1,0:T(8,128)(2,1)} %get-tuple-element.83.mix_rows_h, ...), custom_call_target="tpu_custom_call" | custom-call | tf_op jit(solution)/shard_map/recurrence_back/pallas_call | solution.py:1386
  303.0 52.9 %last.1 = (f32[2,64,2048]{2,1,0:T(8,128)}, f32[256,1664]{1,0:T(8,128)}, f32[3,4,2048]{2,1,0:T(4,128)}, f32[1,128]{1,0:T(1,128)}, f32[1,128]{1,0:T(1,128)}, /*ind...) custom-call(bf16[2,256,2048]{2,1,0:T(8,128)(2,1)} %get-tuple-element.101.rows, ...), custom_call_target="tpu_custom_call" | custom-call | tf_op jit(solution)/shard_map/last/pallas_call | solution.py:1560
  355.9 6.9 %deliver.1 = (f32[2,64,2048]{2,1,0:T(8,128)}, f32[2,64,2048]{2,1,0:T(8,128)}, f32[256,512]{1,0:T(8,128)}, f32[256,512]{1,0:T(8,128)}, f32[256,512]{1,0:T(8,128)}...) custom-call(f32[2,64,2048]{2,1,0:T(8,128)} %get-tuple-element.100.bl, ...), custom_call_target="tpu_custom_call" | custom-call | tf_op jit(solution)/shard_map/deliver/pallas_call | solution.py:1644

commit v2 on v1

--- a/solution.py
+++ b/solution.py
@@ -638,7 +638,7 @@
     proj_shard[:, width : 2 * width] = key_w[...]
     proj_shard[:, 2 * width : 3 * width] = value_w[...]
     proj_shard[:, 3 * width :] = jnp.zeros((proj_shard.shape[0], LANES), BF)
-    proj_shard[:, 3 * width : 3 * width + heads] = beta_w[...]
+    proj_shard[:, 3 * width : 3 * width + heads] = beta_w[...].astype(F32).T.astype(BF)
     out_shard[...] = out_in[...].T
     await_all(mates)
 
@@ -725,10 +725,6 @@
             gates.begin((0,))
             for at in range(NSEQ):
                 spread_grad.begin(at)
-
-        @pl.when(piece == 1)
-        def _():
-            gates.begin(range(1, len(gates.orders[0])))
 
         @pl.when(s > 0)
         def _():
@@ -789,7 +785,8 @@
         run_chains(piece)
 
     def gates_on():
-        gates.advance(4)
+        gates.begin(range(1, len(gates.orders[0])))
+        gates.advance(2)
         ups.begin()
         downs.begin()
 
@@ -841,10 +838,10 @@
         feed_rows[piece, mine, :] = (values * row_scale(values) * feed_gain[...]).astype(BF)
         spread_feed.begin(piece)
 
+    for piece in range(NSEQ):
+        spread_grad.advance(piece, 1)
     apply(0)
     collect.begin(0)
-    for piece in range(NSEQ):
-        spread_grad.advance(piece, 1)
     apply(1, gates_on)
     kept.append((out_w, out_w_o, keep.at[4]))
     later = [
@@ -862,7 +859,7 @@
         collect.advance(0, turn)
     close(0)
     collect.advance(1, 1)
-    gates.advance(2)
+    gates.advance(4)
     spread_feed.advance(0, 0)
     collect.advance(1, 2)
     gates.advance()
@@ -1033,22 +1030,20 @@
     collect.advance(0, 2)
     collect.begin(1)
     weight_grad(feed_rows, grad_up, up_w)
-    first.advance(4)
+    second.begin()
+    first.advance(8)
     for turn in range(3, nm):
         collect.advance(0, turn)
     close(0)
-    first.advance(4)
     collect.advance(1, 1)
-    second.begin()
+    second.advance(8)
     spread.advance(0, 0)
     collect.advance(1, 2)
-    second.advance(8)
+    first.advance(4)
     spread.advance(0, 1)
-    first.advance(2)
     for turn in range(3, nm):
         collect.advance(1, turn)
     close(1)
-    first.advance(2)
     for piece in range(NSEQ):
         collect.finish(piece)
         part[piece] = dot(hidden[piece], down_w[...], NT).astype(BF)
@@ -1056,11 +1051,11 @@
     load(later)
     for hop in range(2, nm - 1):
         spread.advance(0, hop)
+    second.advance(4)
     spread.advance(1, 0)
     weight_grad(grad_rows, hidden, down_w)
     later.append((down_w, grad_down_o, keep.at[1]))
     load(later[1:])
-    second.advance(4)
     for hop in range(1, nm - 1):
         spread.advance(1, hop)
     for piece in range(NSEQ):
@@ -1109,7 +1104,7 @@
     sizes, mix_rows_h, out_weight_h, head_rows, projected, logits, conv, lengths, bias, gain,
     edge, links, solve_h, wkeys_h, fresh_h, error_h, outputs_h, queries_h, keys_h, entry,
     grad_down_hbm, down_part_hbm, hidden_in,
-    grads_o, block_o, grad_out_o, grad_down_o, conv_o, gain_o, bias_o,
+    grads_o, block_o, grad_down_o, conv_o, gain_o, bias_o, out_total_o,
     mix_rows, out_weight, solve, fresh, error, queries, keys,
     extended, betas, grad_output, held, grad_mixed, grad_tail, grad_logit,
     pair, gathered, leaving, edge_out, edge_in, out_total, down_total, down_part, keep,
@@ -1123,6 +1118,7 @@
     which = range(heads)
     mates = line_mates(geo) + all_mates(geo)
     greet(mates)
+    kept = [(out_total, out_total_o, keep.at[11])]
     loads = [
         (down_part_hbm, down_part, keep.at[0]), (grad_down_hbm, down_total, keep.at[1]),
         (mix_rows_h, mix_rows, keep.at[2]), (out_weight_h, out_weight, keep.at[3]),
@@ -1133,8 +1129,7 @@
     load(loads)
     collect = LineScatter(geo, down_part, rest[0:3])
     first = CubeScatter(geo, down_total, rest[3:6])
-    second = CubeScatter(geo, out_total, rest[6:9])
-    chain = Chains(geo, chains, pair, gathered, leaving, rest[9:14])
+    chain = Chains(geo, chains, pair, gathered, leaving, rest[6:11])
     strict = lower_mask(span, True)
     whole = lower_mask(span, False)
     gain_o[...] = jnp.zeros(gain_o.shape, F32)
@@ -1147,9 +1142,10 @@
         strength, live = strengths_of(geo, logits, lengths, bias, heads, piece)
         betas[piece] = strength * live
     await_all(mates)
-    ready(loads[:2])
+    ready(loads[:1])
     for piece in range(NSEQ):
         collect.begin(piece)
+    ready(loads[1:2])
     first.begin()
     ready(loads[2:8])
 
@@ -1187,6 +1183,7 @@
         return carry
 
     lax.fori_loop(0, NSEQ, start, 0)
+    first.advance(2)
     ready(loads[8:])
 
     def through_conv(piece, h, group, grad, key=None):
@@ -1238,6 +1235,11 @@
         base = piece * heads
         for h in which:
             chain.receive(base + h)
+
+        @pl.when(piece == 0)
+        def _():
+            first.advance(6)
+
         key_pairs = [halves(keys[base + h]) for h in which]
         exits = [halves(leaving[base + h]) for h in which]
         fresh_pairs = [halves(fresh[base + h]) for h in which]
@@ -1297,20 +1299,16 @@
         return carry
 
     def leave(piece, carry):
-        @pl.when(piece == 0)
-        def _():
-            first.advance(8)
-
         before_exit(piece)
 
         @pl.when(piece == 0)
         def _():
             for at in range(NSEQ):
                 run_chains(at)
+            lax.fori_loop(0, depth // tile, weight_grad, 0)
+            load(kept)
             for at in range(NSEQ):
                 collect.advance(at, 1)
-            lax.fori_loop(0, depth // tile, weight_grad, 0)
-            second.begin()
 
         return carry
 
@@ -1327,8 +1325,6 @@
         def _():
             for at in range(NSEQ):
                 collect.advance(at, 2)
-            second.advance(8)
-            first.advance(4)
 
         return carry
 
@@ -1344,7 +1340,7 @@
     for h in which:
         spread_bias = spread_bias + jnp.where(lane == m * heads + h, column_of(bias_sum, h), 0.0)
     bias_o[...] = spread_bias
-    second.advance(4)
+    first.advance(4)
     for turn in range(3, nm):
         for piece in range(NSEQ):
             collect.advance(piece, turn)
@@ -1366,8 +1362,8 @@
             edge_copy(piece).wait_send()
 
     first.finish(grad_down_o)
-    second.finish(grad_out_o)
     chain.finish()
+    ready(kept)
 
 
 def backward(
@@ -1388,14 +1384,14 @@
         out_shape=(
             jax.ShapeDtypeStruct((NSEQ, span, 3 * width + LANES), BF),
             jax.ShapeDtypeStruct(local, F32),
-            jax.ShapeDtypeStruct((shard, width), F32),
             jax.ShapeDtypeStruct((shard, cols), F32),
             jax.ShapeDtypeStruct((12, width), F32),
             jax.ShapeDtypeStruct((1, LANES), F32),
             jax.ShapeDtypeStruct((1, LANES), F32),
+            jax.ShapeDtypeStruct((depth, width), BF),
         ),
         in_specs=[ANY, ANY] + [VMEM] * 4 + [SMEM, SMEM] + [VMEM] * 3 + [ANY] * 7 + [VMEM, ANY, ANY, VMEM],
-        out_specs=(VMEM,) * 7,
+        out_specs=(VMEM,) * 6 + (ANY,),
         scratch_shapes=[
             pltpu.VMEM(rows, BF), pltpu.VMEM((depth, width), BF),
             pltpu.VMEM((chains, span, span), F32),
@@ -1417,11 +1413,10 @@
             pltpu.VMEM((depth, width), BF),
             pltpu.VMEM((depth, cols), BF),
             pltpu.VMEM(rows, BF),
-            DMA((11,)), DMA((NSEQ,)), DMA((NSEQ,)),
+            DMA((12,)), DMA((NSEQ,)), DMA((NSEQ,)),
         ]
         + LineScatter.scratch(nm, local[1], depth)
         + CubeScatter.scratch(ns, shard, cols)
-        + CubeScatter.scratch(ns, shard, width)
         + Chains.scratch(ns, chains),
         compiler_params=comm_params(2, 63),
         name="recurrence_back",
@@ -1432,15 +1427,19 @@
 
 
 def last_kernel(
-    sizes, rows, grads, proj_w, tokens, gain, grad_in, conv_part, head_gain, bias, norms, feed_gain,
-    grad_tokens, grad_weight_o, conv_o, head_gain_o, bias_o, norm_o, feed_gain_o, gain_o,
-    part, total, vector, over_seq, over_mp,
-    seq_send, seq_recv, mp_send, mp_recv, *rest,
+    sizes, rows_h, grads, proj_w, out_total_h, tokens, gain, grad_in,
+    conv_part, head_gain, bias, norms, feed_gain,
+    grad_tokens, grad_weight_o, grad_out_o,
+    conv_o, head_gain_o, bias_o, norm_o, feed_gain_o, gain_o,
+    rows, part, total, out_total, vector, over_seq, over_mp,
+    keep, seq_send, seq_recv, mp_send, mp_recv, *rest,
 ):
     geo = Geo(sizes)
     ns, nm, s, m = geo.ns, geo.nm, geo.s, geo.m
     mates = [(s, (m + k) % nm) for k in range(1, nm)] + all_mates(geo)
     greet(mates)
+    loads = [(out_total_h, out_total, keep.at[0]), (rows_h, rows, keep.at[1])]
+    load(loads)
     depth = proj_w.shape[0]
     width = vector.shape[1]
     wide = depth // width
@@ -1455,26 +1454,36 @@
     await_all(mates)
     collect = LineScatter(geo, part, rest[0:3])
     scatter = CubeScatter(geo, total, rest[3:6])
+    outs = CubeScatter(geo, out_total, rest[6:9])
     shares = []
 
     def spread(piece):
         value = dot(grads[piece], proj_w[...], NT)
         part[piece] = value.astype(BF)
         collect.begin(piece)
+        if piece == 0:
+            ready(loads[1:])
         shares.append(jnp.sum(value * rows[piece].astype(F32), 0, keepdims=True))
 
     tile = 512
 
-    def weight_grad(at, carry):
-        window = pl.ds(pl.multiple_of(at * tile, tile), tile)
-        value = dot(rows[0, :, window], grads[0], TN) + dot(rows[1, :, window], grads[1], TN)
-        total[window, :] = value.astype(BF)
-        return carry
-
+    def weight_grad(left, right, out):
+        def step(at, carry):
+            window = pl.ds(pl.multiple_of(at * tile, tile), tile)
+            value = dot(left[0, :, window], right[0], TN) + dot(left[1, :, window], right[1], TN)
+            out[window, :] = value.astype(BF)
+            return carry
+
+        lax.fori_loop(0, depth // tile, step, 0)
+
+    ready(loads[:1])
+    outs.begin()
     spread(0)
-    lax.fori_loop(0, depth // tile, weight_grad, 0)
+    outs.advance(8)
+    weight_grad(rows, grads, total)
     scatter.begin()
     spread(1)
+    outs.advance(2)
     share = (shares[0] + shares[1]) / gain[...]
     for at in range(wide):
         vector[row + 1 + wide + at : row + 2 + wide + at, :] = share[:, at * width : (at + 1) * width]
@@ -1505,13 +1514,16 @@
     for k in range(nm - 1):
         mp_copy(k).start()
     collect.advance(1, 1)
-    for turn in range(2, nm):
-        for piece in range(NSEQ):
-            collect.advance(piece, turn)
-        if turn == 2:
-            for k in range(nm - 1):
-                mp_copy(k).wait_recv()
-            scatter.advance(2)
+    collect.advance(0, 2)
+    outs.advance(2)
+    for k in range(nm - 1):
+        mp_copy(k).wait_recv()
+    scatter.advance(2)
+    collect.advance(1, 2)
+    for turn in range(3, nm):
+        collect.advance(0, turn)
+        scatter.advance(2)
+        collect.advance(1, turn)
     for piece in range(NSEQ):
         collect.result(piece, grad_tokens)
         values = tokens[piece].astype(F32)
@@ -1537,6 +1549,7 @@
         cols = slice(at * width, (at + 1) * width)
         feed_gain_o[:, cols] = summed[row + 1 + at : row + 2 + at, :]
         gain_o[:, cols] = summed[row + 1 + wide + at : row + 2 + wide + at, :]
+    outs.finish(grad_out_o)
     scatter.finish(grad_weight_o)
 
     def seq_done(k, carry):
@@ -1548,7 +1561,7 @@
         mp_copy(k).wait_send()
 
 
-def last(sizes, rows, grads, proj_w, tokens, gain, grad_in, small):
+def last(sizes, rows, grads, proj_w, out_total, tokens, gain, grad_in, small):
     ns, nm = sizes
     depth, cols = proj_w.shape
     span = tokens.shape[1]
@@ -1560,24 +1573,27 @@
     return pl.pallas_call(
         functools.partial(last_kernel, sizes),
         out_shape=(
-            shape(grad_in.shape, F32), shape((shard, cols), F32), shape((3, 4, depth), F32),
-            line, line, line, shape((1, depth), F32), shape((1, depth), F32),
+            shape(grad_in.shape, F32), shape((shard, cols), F32), shape((shard, width), F32),
+            shape((3, 4, depth), F32), line, line, line, shape((1, depth), F32), shape((1, depth), F32),
         ),
-        in_specs=[VMEM] * 11,
-        out_specs=(VMEM,) * 8,
+        in_specs=[ANY, VMEM, VMEM, ANY] + [VMEM] * 8,
+        out_specs=(VMEM,) * 9,
         scratch_shapes=[
             pltpu.VMEM(rows.shape, BF),
+            pltpu.VMEM(rows.shape, BF),
             pltpu.VMEM((depth, cols), BF),
+            pltpu.VMEM((depth, width), BF),
             pltpu.VMEM(vector, F32),
             pltpu.VMEM((ns - 1,) + vector, F32),
             pltpu.VMEM((nm,) + vector, F32),
-            DMA((ns - 1,)), DMA((ns - 1,)), DMA((nm - 1,)), DMA((nm - 1,)),
+            DMA((2,)), DMA((ns - 1,)), DMA((ns - 1,)), DMA((nm - 1,)), DMA((nm - 1,)),
         ]
         + LineScatter.scratch(nm, span, depth)
-        + CubeScatter.scratch(ns, shard, cols),
+        + CubeScatter.scratch(ns, shard, cols)
+        + CubeScatter.scratch(ns, shard, width),
         compiler_params=comm_params(3),
         name="last",
-    )(rows, grads, proj_w, tokens, gain, grad_in, *small)
+    )(rows, grads, proj_w, out_total, tokens, gain, grad_in, *small)
 
 
 def deliver_kernel(
@@ -1687,19 +1703,22 @@
         rows, proj_w, out_w, gate_w, up_w, down_w, grad_rows, feed_rows,
         hidden_in, head_rows, projected, logits, edge, links, norms, entry, *saved,
     ) = mixer(
-        sizes, tokens, cotangent, query_weight, key_weight, value_weight, beta_weight, out_weight,
+        sizes, tokens, cotangent, query_weight, key_weight, value_weight, beta_weight.T, out_weight,
         gate_weight, up_weight, down_weight, conv_weight, lengths, beta_bias, mixer_gain_row,
         head_gain_row, feed_gain_row,
     )
     grad_in, mix_rows, grad_gate, grad_up, grad_down_part, down_part, feed_gain_part = feed(
         sizes, feed_rows, grad_rows, gate_w, up_w, down_w, hidden_in, feed_gain_row, cotangent
     )
-    grads, block_output, grad_out, grad_down, conv_part, gain_part, bias_part = backward(
+    grads, block_output, grad_down, conv_part, gain_part, bias_part, grad_out_part = backward(
         sizes, mix_rows, out_w, head_rows, projected, logits, conv_weight, lengths, beta_bias,
         head_gain_row, (edge, links, *saved, entry), grad_down_part, down_part, hidden_in,
     )
-    grad_tokens, grad_proj_w, conv_grad, gain_grad, bias_grad, norm, feed_gain_grad, mixer_grad = last(
-        sizes, rows, grads, proj_w, tokens, mixer_gain_row, grad_in,
+    (
+        grad_tokens, grad_proj_w, grad_out, conv_grad, gain_grad, bias_grad, norm, feed_gain_grad,
+        mixer_grad,
+    ) = last(
+        sizes, rows, grads, proj_w, grad_out_part, tokens, mixer_gain_row, grad_in,
         (conv_part, gain_part, bias_part, norms, feed_gain_part),
     )
     (

time: 369 us -> 354 us (0.959)
  Pallas kernels: 361 us -> 347 us
    pallas_call x1, Pallas kernels: 62.9 us -> 50.1 us  [backward(): pl.pallas_call(functools.partial(backward_kernel, sizes), out_shape=(jax....]
where the time goes in v2:
time: 354 us; the launch traced here: 348 us
  Pallas kernels  347 us (98%)
    pallas_call x1, Pallas kernels, mixer(): pl.pallas_call(functools.partial(mixer_kernel, sizes), out_shape=(shape(r...  146 us
    pallas_call x1, Pallas kernels, feed(): pl.pallas_call(functools.partial(feed_kernel, sizes), out_shape=(jax.Shap...  87.9 us
    pallas_call x1, Pallas kernels, last(): pl.pallas_call(functools.partial(last_kernel, sizes), out_shape=(shape(gr...  56 us
    pallas_call x1, Pallas kernels, backward(): pl.pallas_call(functools.partial(backward_kernel, sizes), out_shape=(jax....  50.1 us

profile of v2, /device:TPU:0, one launch (start us, length us, event | category | flops | bytes accessed | tf_op | source)
XLA Modules:
  0.0 348.3 jit_solution(17844440862049539048)
XLA Ops:
  0.6 146.1 %mixer.1 = (bf16[2,256,2048]{2,1,0:T(8,128)(2,1)}, bf16[2048,1664]{1,0:T(8,128)(2,1)}, bf16[2048,512]{1,0:T(8,128)(2,1)}, bf16[2048,1408]{1,0:T(8,128)(2,1)}, bf...) custom-call(bf16[2,64,2048]{2,1,0:T(8,128)(2,1)} %tokens.3, ...), custom_call_target="tpu_custom_call" | custom-call | tf_op jit(solution)/shard_map/mixer/pallas_call | solution.py:922
  146.8 87.9 %feed.1 = (f32[2,64,2048]{2,1,0:T(8,128)}, bf16[2,256,2048]{2,1,0:T(8,128)(2,1)}, f32[256,1408]{1,0:T(8,128)}, f32[256,1408]{1,0:T(8,128)}, bf16[2048,1408]{1,0:...) custom-call(bf16[2,256,2048]{2,1,0:T(8,128)(2,1)} %get-tuple-element.78.feed_rows, ...), custom_call_target="tpu_custom_call" | custom-call | tf_op jit(solution)/shard_map/feed/pallas_call | solution.py:1077
  234.7 50.1 %recurrence_back.1 = (bf16[2,256,1664]{2,1,0:T(8,128)(2,1)}, f32[2,64,2048]{2,1,0:T(8,128)}, f32[256,1408]{1,0:T(8,128)}, f32[12,512]{1,0:T(8,128)}, f32[1,128]{...) custom-call(bf16[2,256,2048]{2,1,0:T(8,128)(2,1)} %get-tuple-element.84.mix_rows_h, ...), custom_call_target="tpu_custom_call" | custom-call | tf_op jit(solution)/shard_map/recurrence_back/pallas_call | solution.py:1382
  284.8 56.0 %last.1 = (f32[2,64,2048]{2,1,0:T(8,128)}, f32[256,1664]{1,0:T(8,128)}, f32[256,512]{1,0:T(8,128)}, f32[3,4,2048]{2,1,0:T(4,128)}, f32[1,128]{1,0:T(1,128)}, /*i...) custom-call(bf16[2,256,2048]{2,1,0:T(8,128)(2,1)} %get-tuple-element.102.rows_h, ...), custom_call_target="tpu_custom_call" | custom-call | tf_op jit(solution)/shard_map/last/pallas_call | solution.py:1573
  340.9 6.9 %deliver.1 = (f32[2,64,2048]{2,1,0:T(8,128)}, f32[2,64,2048]{2,1,0:T(8,128)}, f32[256,512]{1,0:T(8,128)}, f32[256,512]{1,0:T(8,128)}, f32[256,512]{1,0:T(8,128)}...) custom-call(f32[2,64,2048]{2,1,0:T(8,128)} %get-tuple-element.101.bl, ...), custom_call_target="tpu_custom_call" | custom-call | tf_op jit(solution)/shard_map/deliver/pallas_call | solution.py:1660

commit v3 on v2

--- a/solution.py
+++ b/solution.py
@@ -873,10 +873,16 @@
         spread_feed.advance(0, hop)
     for piece in range(NSEQ):
         spread_grad.advance(piece, nm - 2)
+    late = [
+        (feed_rows.at[0], feed_rows_o.at[0], keep.at[5]), (grad_rows, grad_rows_o, keep.at[6]),
+        (rows, rows_o, keep.at[3]), (feed_rows.at[1], feed_rows_o.at[1], keep.at[14]),
+    ]
+    load(late[:3])
     spread_feed.advance(1, 0)
     ups.advance(2)
     for hop in range(1, nm - 1):
         spread_feed.advance(1, hop)
+    load(late[3:])
     downs.advance(2)
     ups.advance()
     downs.advance()
@@ -885,10 +891,6 @@
         collect.finish(piece)
         spread_grad.finish(piece)
         spread_feed.finish(piece)
-    late = [
-        (feed_rows, feed_rows_o, keep.at[5]), (grad_rows, grad_rows_o, keep.at[6]), (rows, rows_o, keep.at[3])
-    ]
-    load(late)
     for gather in (gates, ups, downs):
         gather.settle()
     for gather in (weights, outs, gates, ups, downs):
@@ -944,7 +946,7 @@
             pltpu.VMEM((NSEQ, span, LANES), F32),
             pltpu.VMEM(per_chain, F32),
             pltpu.VMEM((chains, LANES, 2 * LANES), BF),
-            DMA((14,)), DMA((NSEQ,)), DMA((NSEQ,)),
+            DMA((15,)), DMA((NSEQ,)), DMA((NSEQ,)),
         ]
         + CubeGather.sems(ns) * 5
         + LineGather.sems(nm) * 3
@@ -959,24 +961,27 @@
 
 
 def feed_kernel(
-    sizes, feed_rows, grad_rows, gate_hbm, up_hbm, down_hbm, hidden_in, gain, cotangent,
+    sizes, feed_rows_h, grad_rows_h, gate_hbm, up_hbm, down_hbm, hidden_in, gain, cotangent,
     grad_in, mix_rows_o, grad_gate_o, grad_up_o, grad_down_o, down_part_o, gain_o,
-    gate_w, up_w, down_w, hidden, grad_gate, grad_up, part, mix_rows, keep, *rest,
+    feed_rows, grad_rows, gate_w, up_w, down_w, hidden, grad_gate, grad_up, part, mix_rows,
+    keep, *rest,
 ):
     geo = Geo(sizes)
     nm = geo.nm
+    mates = line_mates(geo) + cube_mates(geo)
+    greet(mates)
     weights = [
         (gate_hbm, gate_w, keep.at[0]), (up_hbm, up_w, keep.at[1]), (down_hbm, down_w, keep.at[2])
     ]
-    load(weights)
-    meet(line_mates(geo) + cube_mates(geo))
+    inputs = [(feed_rows_h, feed_rows, keep.at[3]), (grad_rows_h, grad_rows, keep.at[4])]
+    load(inputs[:1] + weights[:2] + inputs[1:] + weights[2:])
     collect = LineScatter(geo, part, rest[0:3])
     spread = LineGather(geo, mix_rows, rest[3:5])
     first = CubeScatter(geo, gate_w, rest[5:8])
     second = CubeScatter(geo, up_w, rest[8:11])
     for piece in range(NSEQ):
         if piece == 0:
-            ready(weights[:1])
+            ready(inputs[:1] + weights[:1])
         gate = dot(feed_rows[piece], gate_w[...])
         if piece == 0:
             ready(weights[1:2])
@@ -985,7 +990,7 @@
         active = gate * sig
         hidden[piece] = (active * up).astype(BF)
         if piece == 0:
-            ready(weights[2:3])
+            ready(inputs[1:] + weights[2:])
         grad_hidden = dot(grad_rows[piece], down_w[...])
         grad_gate[piece] = (grad_hidden * up * sig * (1.0 + gate * (1.0 - sig))).astype(BF)
         grad_up[piece] = (grad_hidden * active).astype(BF)
@@ -993,6 +998,7 @@
             dot(grad_gate[piece], gate_w[...], NT) + dot(grad_up[piece], up_w[...], NT)
         ).astype(BF)
         if piece == 0:
+            await_all(mates)
             collect.begin(0)
     depth, cols = gate_w.shape
     tile = 512
@@ -1085,12 +1091,13 @@
             jax.ShapeDtypeStruct(rows, BF),
             jax.ShapeDtypeStruct((1, depth), F32),
         ),
-        in_specs=[VMEM, VMEM, ANY, ANY, ANY, VMEM, VMEM, VMEM],
+        in_specs=[ANY] * 5 + [VMEM] * 3,
         out_specs=(VMEM, ANY, VMEM, VMEM, ANY, ANY, VMEM),
         scratch_shapes=[
+            pltpu.VMEM(rows, BF), pltpu.VMEM(rows, BF),
             pltpu.VMEM((depth, cols), BF), pltpu.VMEM((depth, cols), BF), pltpu.VMEM((depth, cols), BF),
             pltpu.VMEM(inner, BF), pltpu.VMEM(inner, BF), pltpu.VMEM(inner, BF),
-            pltpu.VMEM(rows, BF), pltpu.VMEM(rows, BF), DMA((3,)),
+            pltpu.VMEM(rows, BF), pltpu.VMEM(rows, BF), DMA((5,)),
         ]
         + LineScatter.scratch(nm, span, depth)
         + LineGather.sems(nm)
@@ -1427,19 +1434,22 @@
 
 
 def last_kernel(
-    sizes, rows_h, grads, proj_w, out_total_h, tokens, gain, grad_in,
+    sizes, rows_h, grads_h, proj_w_h, out_total_h, tokens, gain, grad_in,
     conv_part, head_gain, bias, norms, feed_gain,
     grad_tokens, grad_weight_o, grad_out_o,
     conv_o, head_gain_o, bias_o, norm_o, feed_gain_o, gain_o,
-    rows, part, total, out_total, vector, over_seq, over_mp,
+    rows, grads, proj_w, part, total, out_total, vector, over_seq, over_mp,
     keep, seq_send, seq_recv, mp_send, mp_recv, *rest,
 ):
     geo = Geo(sizes)
     ns, nm, s, m = geo.ns, geo.nm, geo.s, geo.m
     mates = [(s, (m + k) % nm) for k in range(1, nm)] + all_mates(geo)
     greet(mates)
-    loads = [(out_total_h, out_total, keep.at[0]), (rows_h, rows, keep.at[1])]
-    load(loads)
+    loads = [
+        (out_total_h, out_total, keep.at[0]), (rows_h, rows, keep.at[1]), (grads_h, grads, keep.at[2]),
+        (proj_w_h, proj_w, keep.at[3]),
+    ]
+    load(loads[2:] + loads[:2])
     depth = proj_w.shape[0]
     width = vector.shape[1]
     wide = depth // width
@@ -1458,11 +1468,13 @@
     shares = []
 
     def spread(piece):
+        if piece == 0:
+            ready(loads[2:])
         value = dot(grads[piece], proj_w[...], NT)
         part[piece] = value.astype(BF)
         collect.begin(piece)
         if piece == 0:
-            ready(loads[1:])
+            ready(loads[1:2])
         shares.append(jnp.sum(value * rows[piece].astype(F32), 0, keepdims=True))
 
     tile = 512
@@ -1576,17 +1588,19 @@
             shape(grad_in.shape, F32), shape((shard, cols), F32), shape((shard, width), F32),
             shape((3, 4, depth), F32), line, line, line, shape((1, depth), F32), shape((1, depth), F32),
         ),
-        in_specs=[ANY, VMEM, VMEM, ANY] + [VMEM] * 8,
+        in_specs=[ANY] * 4 + [VMEM] * 8,
         out_specs=(VMEM,) * 9,
         scratch_shapes=[
             pltpu.VMEM(rows.shape, BF),
+            pltpu.VMEM(grads.shape, BF),
+            pltpu.VMEM((depth, cols), BF),
             pltpu.VMEM(rows.shape, BF),
             pltpu.VMEM((depth, cols), BF),
             pltpu.VMEM((depth, width), BF),
             pltpu.VMEM(vector, F32),
             pltpu.VMEM((ns - 1,) + vector, F32),
             pltpu.VMEM((nm,) + vector, F32),
-            DMA((2,)), DMA((ns - 1,)), DMA((ns - 1,)), DMA((nm - 1,)), DMA((nm - 1,)),
+            DMA((4,)), DMA((ns - 1,)), DMA((ns - 1,)), DMA((nm - 1,)), DMA((nm - 1,)),
         ]
         + LineScatter.scratch(nm, span, depth)
         + CubeScatter.scratch(ns, shard, cols)
@@ -1612,8 +1626,8 @@
         (src, held, sems.at[k])
         for k, (src, held) in enumerate(
             (
-                (grad_down, down_v), (grad_out, out_v), (grad_gate, gate_v), (grad_up, up_v),
-                (block, block_v), (grad_tokens, tokens_v), (grad_proj, proj_v), (conv, conv_v),
+                (grad_gate, gate_v), (grad_up, up_v), (block, block_v), (grad_tokens, tokens_v),
+                (grad_proj, proj_v), (grad_out, out_v), (grad_down, down_v), (conv, conv_v),
             )
             + tuple(zip(lines, line_vs))
         )
@@ -1625,19 +1639,19 @@
         going.append((held, dst, sems.at[len(coming) + len(going)]))
         load(going[-1:])
 
-    ready(coming[0:2])
-    down_t[...] = down_v[...].T
-    send(down_t, grad_down_o)
-    out_t[...] = out_v[...].T
-    send(out_t, grad_out_o)
-    ready(coming[2:6])
+    ready(coming[0:4])
     send(gate_v, grad_gate_o)
     send(up_v, grad_up_o)
     send(block_v, block_o)
     send(tokens_v, grad_tokens_o)
-    ready(coming[6:])
+    ready(coming[4:5])
     for k, dst in enumerate((query_o, key_o, value_o)):
         send(proj_v.at[:, pl.ds(k * width, width)], dst)
+    ready(coming[5:])
+    out_t[...] = out_v[...].T
+    send(out_t, grad_out_o)
+    down_t[...] = down_v[...].T
+    send(down_t, grad_down_o)
     beta_o[...] = proj_v[:, 3 * width :].T[: beta_o.shape[0], :]
     conv_o[...] = conv_v[...]
     for line, dst in zip(line_vs, line_os):

time: 354 us -> 352 us (level)
  no operation moved by 1% of the time
where the time goes in v3:
time: 352 us; the launch traced here: 346 us
  Pallas kernels  344 us (98%)
    pallas_call x1, Pallas kernels, mixer(): pl.pallas_call(functools.partial(mixer_kernel, sizes), out_shape=(shape(r...  146 us
    pallas_call x1, Pallas kernels, feed(): pl.pallas_call(functools.partial(feed_kernel, sizes), out_shape=(jax.Shap...  86.8 us
    pallas_call x1, Pallas kernels, last(): pl.pallas_call(functools.partial(last_kernel, sizes), out_shape=(shape(gr...  55 us
    pallas_call x1, Pallas kernels, backward(): pl.pallas_call(functools.partial(backward_kernel, sizes), out_shape=(jax....  49.8 us

profile of v3, /device:TPU:0, one launch (start us, length us, event | category | flops | bytes accessed | tf_op | source)
XLA Modules:
  0.0 345.6 jit_solution(9874087723855527374)
XLA Ops:
  0.6 146.1 %mixer.1 = (bf16[2,256,2048]{2,1,0:T(8,128)(2,1)}, bf16[2048,1664]{1,0:T(8,128)(2,1)}, bf16[2048,512]{1,0:T(8,128)(2,1)}, bf16[2048,1408]{1,0:T(8,128)(2,1)}, bf...) custom-call(bf16[2,64,2048]{2,1,0:T(8,128)(2,1)} %tokens.3, ...), custom_call_target="tpu_custom_call" | custom-call | tf_op jit(solution)/shard_map/mixer/pallas_call | solution.py:924
  146.8 86.8 %feed.1 = (f32[2,64,2048]{2,1,0:T(8,128)}, bf16[2,256,2048]{2,1,0:T(8,128)(2,1)}, f32[256,1408]{1,0:T(8,128)}, f32[256,1408]{1,0:T(8,128)}, bf16[2048,1408]{1,0:...) custom-call(bf16[2,256,2048]{2,1,0:T(8,128)(2,1)} %get-tuple-element.78.feed_rows_h, ...), custom_call_target="tpu_custom_call" | custom-call | tf_op jit(solution)/shard_map/feed/pallas_call | solution.py:1083
  233.6 49.8 %recurrence_back.1 = (bf16[2,256,1664]{2,1,0:T(8,128)(2,1)}, f32[2,64,2048]{2,1,0:T(8,128)}, f32[256,1408]{1,0:T(8,128)}, f32[12,512]{1,0:T(8,128)}, f32[1,128]{...) custom-call(bf16[2,256,2048]{2,1,0:T(8,128)(2,1)} %get-tuple-element.84.mix_rows_h, ...), custom_call_target="tpu_custom_call" | custom-call | tf_op jit(solution)/shard_map/recurrence_back/pallas_call | solution.py:1389
  283.4 55.0 %last.1 = (f32[2,64,2048]{2,1,0:T(8,128)}, f32[256,1664]{1,0:T(8,128)}, f32[256,512]{1,0:T(8,128)}, f32[3,4,2048]{2,1,0:T(4,128)}, f32[1,128]{1,0:T(1,128)}, /*i...) custom-call(bf16[2,256,2048]{2,1,0:T(8,128)(2,1)} %get-tuple-element.102.rows_h, ...), custom_call_target="tpu_custom_call" | custom-call | tf_op jit(solution)/shard_map/last/pallas_call | solution.py:1585
  338.4 6.7 %deliver.1 = (f32[2,64,2048]{2,1,0:T(8,128)}, f32[2,64,2048]{2,1,0:T(8,128)}, f32[256,512]{1,0:T(8,128)}, f32[256,512]{1,0:T(8,128)}, f32[256,512]{1,0:T(8,128)}...) custom-call(f32[2,64,2048]{2,1,0:T(8,128)} %get-tuple-element.101.bl, ...), custom_call_target="tpu_custom_call" | custom-call | tf_op jit(solution)/shard_map/deliver/pallas_call | solution.py:1674

commit v4 on v3

--- a/solution.py
+++ b/solution.py
@@ -1454,6 +1454,7 @@
     width = vector.shape[1]
     wide = depth // width
     row = conv_part.shape[0]
+    early = -(-(row + 1 + wide) // 8) * 8
     vector[...] = jnp.zeros(vector.shape, F32)
     vector[0:row, :] = conv_part[...]
     vector[row : row + 1, 0:LANES] = head_gain[...]
@@ -1462,6 +1463,22 @@
     for at in range(wide):
         vector[row + 1 + at : row + 2 + at, :] = feed_gain[:, at * width : (at + 1) * width]
     await_all(mates)
+
+    def seq_copy(stage, k):
+        rows_of = pl.ds(0, early) if stage == 0 else pl.ds(early, vector.shape[0] - early)
+        return remote(
+            vector.at[rows_of], over_seq.at[k, rows_of], seq_send.at[stage, k], seq_recv.at[stage, k],
+            ((s + 1 + k) % ns, m),
+        )
+
+    def seq_start(stage):
+        def step(k, carry):
+            seq_copy(stage, k).start()
+            return carry
+
+        lax.fori_loop(0, ns - 1, step, 0)
+
+    seq_start(0)
     collect = LineScatter(geo, part, rest[0:3])
     scatter = CubeScatter(geo, total, rest[3:6])
     outs = CubeScatter(geo, out_total, rest[6:9])
@@ -1498,28 +1515,20 @@
     outs.advance(2)
     share = (shares[0] + shares[1]) / gain[...]
     for at in range(wide):
-        vector[row + 1 + wide + at : row + 2 + wide + at, :] = share[:, at * width : (at + 1) * width]
-
-    def seq_copy(k):
-        return remote(
-            vector, over_seq.at[k], seq_send.at[k], seq_recv.at[k], ((s + 1 + k) % ns, m)
-        )
+        vector[early + at : early + 1 + at, :] = share[:, at * width : (at + 1) * width]
 
     def mp_copy(k):
         return remote(
             over_mp.at[0], over_mp.at[1 + k], mp_send.at[k], mp_recv.at[k], (s, (m + 1 + k) % nm)
         )
 
-    def seq_start(k, carry):
-        seq_copy(k).start()
-        return carry
-
-    lax.fori_loop(0, ns - 1, seq_start, 0)
+    seq_start(1)
     collect.advance(0, 1)
     scatter.advance(8)
 
     def seq_add(k, value):
-        seq_copy(k).wait_recv()
+        for stage in range(2):
+            seq_copy(stage, k).wait_recv()
         return value + over_seq[k]
 
     over_mp[0] = lax.fori_loop(0, ns - 1, seq_add, vector[...])
@@ -1560,12 +1569,13 @@
     for at in range(wide):
         cols = slice(at * width, (at + 1) * width)
         feed_gain_o[:, cols] = summed[row + 1 + at : row + 2 + at, :]
-        gain_o[:, cols] = summed[row + 1 + wide + at : row + 2 + wide + at, :]
+        gain_o[:, cols] = summed[early + at : early + 1 + at, :]
     outs.finish(grad_out_o)
     scatter.finish(grad_weight_o)
 
     def seq_done(k, carry):
-        seq_copy(k).wait_send()
+        for stage in range(2):
+            seq_copy(stage, k).wait_send()
         return carry
 
     lax.fori_loop(0, ns - 1, seq_done, 0)
@@ -1579,7 +1589,8 @@
     span = tokens.shape[1]
     shard = depth // ns
     width = (cols - LANES) // 3
-    vector = (-(-(13 + 2 * (depth // width)) // 8) * 8, width)
+    wide = depth // width
+    vector = (-(-(13 + wide) // 8) * 8 + -(-wide // 8) * 8, width)
     shape = jax.ShapeDtypeStruct
     line = shape((1, LANES), F32)
     return pl.pallas_call(
@@ -1600,7 +1611,7 @@
             pltpu.VMEM(vector, F32),
             pltpu.VMEM((ns - 1,) + vector, F32),
             pltpu.VMEM((nm,) + vector, F32),
-            DMA((4,)), DMA((ns - 1,)), DMA((ns - 1,)), DMA((nm - 1,)), DMA((nm - 1,)),
+            DMA((4,)), DMA((2, ns - 1)), DMA((2, ns - 1)), DMA((nm - 1,)), DMA((nm - 1,)),
         ]
         + LineScatter.scratch(nm, span, depth)
         + CubeScatter.scratch(ns, shard, cols)

time: 352 us -> 349 us (level)
  no operation moved by 1% of the time
where the time goes in v4:
time: 349 us; the launch traced here: 343 us
  Pallas kernels  342 us (98%)
    pallas_call x1, Pallas kernels, mixer(): pl.pallas_call(functools.partial(mixer_kernel, sizes), out_shape=(shape(r...  146 us
    pallas_call x1, Pallas kernels, feed(): pl.pallas_call(functools.partial(feed_kernel, sizes), out_shape=(jax.Shap...  86.8 us
    pallas_call x1, Pallas kernels, last(): pl.pallas_call(functools.partial(last_kernel, sizes), out_shape=(shape(gr...  52.4 us
    pallas_call x1, Pallas kernels, backward(): pl.pallas_call(functools.partial(backward_kernel, sizes), out_shape=(jax....  49.8 us

profile of v4, /device:TPU:0, one launch (start us, length us, event | category | flops | bytes accessed | tf_op | source)
XLA Modules:
  0.0 342.9 jit_solution(12605974841339819973)
XLA Ops:
  0.6 146.1 %mixer.1 = (bf16[2,256,2048]{2,1,0:T(8,128)(2,1)}, bf16[2048,1664]{1,0:T(8,128)(2,1)}, bf16[2048,512]{1,0:T(8,128)(2,1)}, bf16[2048,1408]{1,0:T(8,128)(2,1)}, bf...) custom-call(bf16[2,64,2048]{2,1,0:T(8,128)(2,1)} %tokens.3, ...), custom_call_target="tpu_custom_call" | custom-call | tf_op jit(solution)/shard_map/mixer/pallas_call | solution.py:924
  146.8 86.8 %feed.1 = (f32[2,64,2048]{2,1,0:T(8,128)}, bf16[2,256,2048]{2,1,0:T(8,128)(2,1)}, f32[256,1408]{1,0:T(8,128)}, f32[256,1408]{1,0:T(8,128)}, bf16[2048,1408]{1,0:...) custom-call(bf16[2,256,2048]{2,1,0:T(8,128)(2,1)} %get-tuple-element.78.feed_rows_h, ...), custom_call_target="tpu_custom_call" | custom-call | tf_op jit(solution)/shard_map/feed/pallas_call | solution.py:1083
  233.6 49.8 %recurrence_back.1 = (bf16[2,256,1664]{2,1,0:T(8,128)(2,1)}, f32[2,64,2048]{2,1,0:T(8,128)}, f32[256,1408]{1,0:T(8,128)}, f32[12,512]{1,0:T(8,128)}, f32[1,128]{...) custom-call(bf16[2,256,2048]{2,1,0:T(8,128)(2,1)} %get-tuple-element.84.mix_rows_h, ...), custom_call_target="tpu_custom_call" | custom-call | tf_op jit(solution)/shard_map/recurrence_back/pallas_call | solution.py:1389
  283.4 52.4 %last.1 = (f32[2,64,2048]{2,1,0:T(8,128)}, f32[256,1664]{1,0:T(8,128)}, f32[256,512]{1,0:T(8,128)}, f32[3,4,2048]{2,1,0:T(4,128)}, f32[1,128]{1,0:T(1,128)}, /*i...) custom-call(bf16[2,256,2048]{2,1,0:T(8,128)(2,1)} %get-tuple-element.102.rows_h, ...), custom_call_target="tpu_custom_call" | custom-call | tf_op jit(solution)/shard_map/last/pallas_call | solution.py:1596
  335.8 6.7 %deliver.1 = (f32[2,64,2048]{2,1,0:T(8,128)}, f32[2,64,2048]{2,1,0:T(8,128)}, f32[256,512]{1,0:T(8,128)}, f32[256,512]{1,0:T(8,128)}, f32[256,512]{1,0:T(8,128)}...) custom-call(f32[2,64,2048]{2,1,0:T(8,128)} %get-tuple-element.101.bl, ...), custom_call_target="tpu_custom_call" | custom-call | tf_op jit(solution)/shard_map/deliver/pallas_call | solution.py:1685
